TPU v7x, 128 devices: a whole 4x4x4 slice. The times are simulated.
128 devices in a mesh: dp: 16 (over x, y), seq: 8 (over z, core).
Axes of the slice: x: 4, y: 4, z: 4, core: 2. Of those that a mesh axis runs over, the one named last changes fastest.
Arguments:
- queries: bfloat16 [32, 512, 5120], P('dp', 'seq'), may hold values from -50 to 50
- key_rows: bfloat16 [32, 512, 1024], P('dp', 'seq'), may hold values from -6 to 6
- value_rows: bfloat16 [32, 512, 1024], P('dp', 'seq'), may hold values from -6 to 6
- cotangent: bfloat16 [32, 512, 5120], P('dp', 'seq'), may hold values from -6 to 6
- episodes: int32 [32, 512], P('dp', 'seq'), may hold values from 0 to 7, never falling along the last dimension, each value on 1 to 341 neighbouring positions
- send_slot: int32 [16], P('dp'), may hold values from 0 to 1
- swap_mask: int32 [1], replicated, may hold values from 1 to 15
Outputs:
- grad_queries: bfloat16 [32, 512, 5120], P('dp', 'seq')
- grad_keys: bfloat16 [32, 512, 1024], P('dp', 'seq')
- grad_values: bfloat16 [32, 512, 1024], P('dp', 'seq')
Inputs may be any that keep to these rules, and one draw needn't show every extreme that they name: `episodes`: episode ids never fall along a span.
All inputs are finite; a program needn't handle non-finite values.
Results may differ from a plain program's by a relative error of at most 0.0055.
Values may be sent and summed in bfloat16 or wider, within the bound.
No kernel may reach another device: no remote copies, remote signals or barrier semaphores. Data moves between devices by JAX's collectives and lax.ppermute only.
A program may use at most 64 MiB of HBM per device.

v0:
```python
import functools
import math

import jax
import jax.numpy as jnp
from jax import lax
from jax.experimental import pallas as pl
from jax.experimental.pallas import tpu as pltpu
from jax.sharding import PartitionSpec as P

H = 40
KVH = 8
DH = 128
GROUPS = H // KVH
LOCAL_KV = KVH // 2
CHIPS = 4
TOK = 64
CHUNK = 2 * TOK
KEYS = CHIPS * CHUNK
QW = H * DH // 2
KW = LOCAL_KV * DH
KVW = 2 * KW
ROWS_Q = GROUPS * CHUNK
SCALE = 1.0 / math.sqrt(DH)
SCALE2 = SCALE * math.log2(math.e)
BF = jnp.bfloat16
F32 = jnp.float32
VMEM_LIMIT = 16 * 1024 * 1024
SMALL_LIMIT = 8 * 1024 * 1024


def interleave(out, rows, k, v):
    for g in range(LOCAL_KV):
        out[rows, 2 * g * DH : (2 * g + 1) * DH] = k[:, g * DH : (g + 1) * DH]
        out[rows, (2 * g + 1) * DH : (2 * g + 2) * DH] = v[:, g * DH : (g + 1) * DH]


def core_of(pos):
    return pos[0] & 1


def span_of(slot, i):
    return slot[0] ^ i


def id_tile(ids, slot, i):
    e = jnp.where(span_of(slot, i) == 0, ids[0:1, :], ids[1:2, :]).astype(F32)
    return jnp.broadcast_to(jnp.concatenate([e, e], axis=1), (16, DH))


def pack_kv_kernel(pos, slot, k, v, ids, out):
    for i in range(2):
        span = span_of(slot, i)
        interleave(out.at[i], slice(0, TOK), k.at[span], v.at[span])
        out[i, TOK : TOK + 16, 0:DH] = id_tile(ids, slot, i).astype(BF)


def pack_kv(where, key_rows, value_rows, episodes):
    return pl.pallas_call(
        pack_kv_kernel,
        grid_spec=pltpu.PrefetchScalarGridSpec(
            num_scalar_prefetch=2,
            grid=(1,),
            in_specs=[
                pl.BlockSpec((2, TOK, KW), lambda i, p, s: (0, 0, 1 - core_of(p))),
                pl.BlockSpec((2, TOK, KW), lambda i, p, s: (0, 0, 1 - core_of(p))),
                pl.BlockSpec((2, TOK), lambda i, p, s: (0, 0)),
            ],
            out_specs=pl.BlockSpec((2, TOK + 16, KVW), lambda i, p, s: (0, 0, 0)),
        ),
        out_shape=jax.ShapeDtypeStruct((2, TOK + 16, KVW), BF),
        cost_estimate=pl.CostEstimate(flops=0, bytes_accessed=1 << 20, transcendentals=0),
        compiler_params=pltpu.CompilerParams(vmem_limit_bytes=SMALL_LIMIT),
        name="pack_kv",
    )(*where, key_rows, value_rows, episodes)


def pack_q_kernel(pos, slot, q, c, out):
    out[0, 0] = q[0]
    out[0, 1] = c[0]


def pack_q(where, queries, cotangent):
    column = lambda i, p, s: (span_of(s, i), 0, 1 - core_of(p))
    return pl.pallas_call(
        pack_q_kernel,
        grid_spec=pltpu.PrefetchScalarGridSpec(
            num_scalar_prefetch=2,
            grid=(2,),
            in_specs=[pl.BlockSpec((1, TOK, QW), column)] * 2,
            out_specs=pl.BlockSpec((1, 2, TOK, QW), lambda i, p, s: (i, 0, 0, 0)),
        ),
        out_shape=jax.ShapeDtypeStruct((2, 2, TOK, QW), BF),
        cost_estimate=pl.CostEstimate(flops=0, bytes_accessed=3 << 20, transcendentals=0),
        compiler_params=pltpu.CompilerParams(vmem_limit_bytes=SMALL_LIMIT),
        name="pack_q",
    )(*where, queries, cotangent)


def chunks_kernel(pos, slot, k, v, ids, got, out_h, out_k):
    first = lax.broadcasted_iota(jnp.int32, (16, DH), 1) < TOK
    for i, out in enumerate((out_h, out_k)):
        span = span_of(slot, i)
        interleave(out, slice(0, TOK), k.at[span], v.at[span])
        out[TOK:CHUNK, :] = got[i, :TOK, :]
        theirs = got[i, TOK : TOK + 16, 0:DH].astype(F32)
        both = jnp.where(first, id_tile(ids, slot, i), theirs).astype(BF)
        out_h[CHUNK : CHUNK + 16, i * DH : (i + 1) * DH] = both


def make_chunks(where, key_rows, value_rows, episodes, got):
    own = pl.BlockSpec((2, TOK, KW), lambda i, p, s: (0, 0, core_of(p)))
    return pl.pallas_call(
        chunks_kernel,
        grid_spec=pltpu.PrefetchScalarGridSpec(
            num_scalar_prefetch=2,
            grid=(1,),
            in_specs=[
                own,
                own,
                pl.BlockSpec((2, TOK), lambda i, p, s: (0, 0)),
                pl.BlockSpec((2, TOK + 16, KVW), lambda i, p, s: (0, 0, 0)),
            ],
            out_specs=[
                pl.BlockSpec((CHUNK + 16, KVW), lambda i, p, s: (0, 0)),
                pl.BlockSpec((CHUNK, KVW), lambda i, p, s: (0, 0)),
            ],
        ),
        out_shape=[
            jax.ShapeDtypeStruct((CHUNK + 16, KVW), BF),
            jax.ShapeDtypeStruct((CHUNK, KVW), BF),
        ],
        cost_estimate=pl.CostEstimate(flops=0, bytes_accessed=2 << 20, transcendentals=0),
        compiler_params=pltpu.CompilerParams(vmem_limit_bytes=SMALL_LIMIT),
        name="make_chunks",
    )(*where, key_rows, value_rows, episodes, got)


def attention_kernel(
    pos, slot, qo, co, qx, k0, k1, k2, k3, i0, i1, i2, i3,
    gqo, gqx, p0, p1, p2, p3, bias, st, dt, pt, ds,
):
    chip = pos[0] >> 1
    core = core_of(pos)

    @pl.when(pl.program_id(0) == 0)
    def _():
        rows = lax.broadcasted_iota(jnp.int32, (CHUNK, CHUNK), 0)
        lanes = lax.broadcasted_iota(jnp.int32, (CHUNK, CHUNK), 1)
        query_pos = chip * CHUNK + ((lanes + core * TOK) & (CHUNK - 1))
        query_id = jnp.broadcast_to(i0[0:1, :].astype(F32), (CHUNK, CHUNK))
        for d, ids in enumerate((i0, i1, i2, i3)):
            key_pos = ((chip - d) & (CHIPS - 1)) * CHUNK + ((rows + core * TOK) & (CHUNK - 1))
            key_id = jnp.broadcast_to(ids[0:1, :].astype(F32), (CHUNK, CHUNK)).T
            allowed = (key_id == query_id) & (key_pos <= query_pos)
            bias[d * CHUNK : (d + 1) * CHUNK, :] = jnp.where(allowed, 0.0, -1e30).astype(F32)

    kv = [k[0:CHUNK, :] for k in (k0, k1, k2, k3)]
    keys = jnp.concatenate([x[:, :DH] for x in kv], axis=0)
    values = jnp.concatenate([x[:, DH:] for x in kv], axis=0)

    def heads(own, other):
        parts = []
        for h in range(GROUPS):
            parts.append(own[:, h * DH : (h + 1) * DH])
            parts.append(other[:, h * DH : (h + 1) * DH])
        return jnp.concatenate(parts, axis=0)

    queries = heads(qo[0], qx[0, 0])
    cots = heads(co[0], qx[0, 1])
    last = (((1,), (1,)), ((), ()))
    st[...] = lax.dot_general(keys, queries, last, preferred_element_type=F32)
    dt[...] = lax.dot_general(values, cots, last, preferred_element_type=F32)
    for h in range(GROUPS):
        cut = slice(h * CHUNK, (h + 1) * CHUNK)
        s = st[:, cut] * SCALE2 + bias[...]
        top = jnp.max(s, axis=0, keepdims=True)
        e = jnp.exp2(s - top)
        probs = e * (1.0 / jnp.sum(e, axis=0, keepdims=True))
        dprobs = dt[:, cut]
        delta = jnp.sum(probs * dprobs, axis=0, keepdims=True)
        pt[:, cut] = probs.astype(BF)
        ds[:, cut] = (probs * (dprobs - delta)).astype(BF)
    grad_k = jnp.dot(ds[...], queries, preferred_element_type=F32) * SCALE
    grad_v = jnp.dot(pt[...], cots, preferred_element_type=F32)
    for d, p in enumerate((p0, p1, p2, p3)):
        cut = slice(d * CHUNK, (d + 1) * CHUNK)
        p[:, :DH] = grad_k[cut].astype(p.dtype)
        p[:, DH:] = grad_v[cut].astype(p.dtype)
    gq_t = jnp.dot(keys.T, ds[...], preferred_element_type=F32) * SCALE
    for h in range(GROUPS):
        gq = gq_t[:, h * CHUNK : (h + 1) * CHUNK].T.astype(BF)
        gqo[:, h * DH : (h + 1) * DH] = gq[:TOK]
        gqx[:, h * DH : (h + 1) * DH] = gq[TOK:]


def attention(where, which, queries, cotangent, q_other, chunks, id_chunks):
    own = pl.BlockSpec((1, TOK, GROUPS * DH), lambda g, p, s: (span_of(s, which), 0, core_of(p) * LOCAL_KV + g))
    other = pl.BlockSpec((1, 2, TOK, GROUPS * DH), lambda g, p, s: (which, 0, 0, g))
    chunk = pl.BlockSpec((CHUNK, 2 * DH), lambda g, p, s: (0, g))
    ids = pl.BlockSpec((16, DH), lambda g, p, s: (CHUNK // 16, which))
    out_q = pl.BlockSpec((TOK, GROUPS * DH), lambda g, p, s: (0, g))
    return pl.pallas_call(
        attention_kernel,
        grid_spec=pltpu.PrefetchScalarGridSpec(
            num_scalar_prefetch=2,
            grid=(LOCAL_KV,),
            in_specs=[own, own, other] + [chunk] * 4 + [ids] * 4,
            out_specs=[out_q, out_q] + [chunk] * 4,
            scratch_shapes=[
                pltpu.VMEM((KEYS, CHUNK), F32),
                pltpu.VMEM((KEYS, ROWS_Q), F32),
                pltpu.VMEM((KEYS, ROWS_Q), F32),
                pltpu.VMEM((KEYS, ROWS_Q), BF),
                pltpu.VMEM((KEYS, ROWS_Q), BF),
            ],
        ),
        out_shape=[jax.ShapeDtypeStruct((TOK, QW), BF)] * 2
        + [jax.ShapeDtypeStruct((CHUNK, KVW), F32)]
        + [jax.ShapeDtypeStruct((CHUNK, KVW), BF)] * 3,
        compiler_params=pltpu.CompilerParams(
            dimension_semantics=("arbitrary",), vmem_limit_bytes=VMEM_LIMIT
        ),
        cost_estimate=pl.CostEstimate(
            flops=10 * KEYS * ROWS_Q * DH * LOCAL_KV,
            bytes_accessed=5 << 20,
            transcendentals=KEYS * ROWS_Q * LOCAL_KV,
        ),
        name="attention",
    )(*where, queries, cotangent, q_other, *chunks, *id_chunks)


def total_of(p0, r1, r2, r3):
    total = (p0[...] + r1[...].astype(F32)) + (r2[...].astype(F32) + r3[...].astype(F32))
    return total.astype(BF)


def hand_over_kernel(p0, r1, r2, r3, gq_own, gq_got, out):
    total = total_of(p0, r1, r2, r3)
    out[:, 0:QW] = gq_own[...]
    out[:, QW : 2 * QW] = gq_got[...]
    out[:, 2 * QW : 2 * QW + KVW] = total[:TOK]
    out[:, 2 * QW + KVW :] = total[TOK:]


def hand_over(parts, gq_own, gq_got):
    return pl.pallas_call(
        hand_over_kernel,
        out_shape=jax.ShapeDtypeStruct((TOK, 2 * QW + 2 * KVW), BF),
        compiler_params=pltpu.CompilerParams(vmem_limit_bytes=SMALL_LIMIT),
        cost_estimate=pl.CostEstimate(flops=0, bytes_accessed=4 << 20, transcendentals=0),
        name="hand_over",
    )(*parts, gq_own, gq_got)


def keep_kernel(p0, r1, r2, r3, new, own, swap):
    total = total_of(p0, r1, r2, r3)
    own[...] = total[:TOK]
    swap[:, :KVW] = total[TOK:]
    swap[:, KVW:] = new[...]


def keep(parts, new):
    whole = lambda shape: pl.BlockSpec(shape, lambda i: (0, 0))
    return pl.pallas_call(
        keep_kernel,
        grid=(1,),
        in_specs=[whole((CHUNK, KVW))] * 4
        + [pl.BlockSpec((TOK, KVW), lambda i: (0, 2 * QW // KVW + 1))],
        out_specs=[whole((TOK, KVW)), whole((TOK, 2 * KVW))],
        out_shape=[
            jax.ShapeDtypeStruct((TOK, KVW), BF),
            jax.ShapeDtypeStruct((TOK, 2 * KVW), BF),
        ],
        compiler_params=pltpu.CompilerParams(vmem_limit_bytes=SMALL_LIMIT),
        cost_estimate=pl.CostEstimate(flops=0, bytes_accessed=2 << 20, transcendentals=0),
        name="keep",
    )(*parts, new)


def place_q_kernel(pos, slot, kept_own, kept_other, new, out):
    for core in range(2):

        @pl.when(core_of(pos) == core)
        def _():
            a = slice(core * QW, (core + 1) * QW)
            b = slice((1 - core) * QW, (2 - core) * QW)
            out[0, :, a] = kept_own[...]
            out[0, :, b] = kept_other[...]
            out[1, :, a] = new[:, :QW]
            out[1, :, b] = new[:, QW:]


def place_q(where, kept_own, kept_other, new):
    return pl.pallas_call(
        place_q_kernel,
        grid_spec=pltpu.PrefetchScalarGridSpec(
            num_scalar_prefetch=2,
            grid=(1,),
            in_specs=[pl.BlockSpec((TOK, QW), lambda i, p, s: (0, 0))] * 2
            + [pl.BlockSpec((TOK, 2 * QW), lambda i, p, s: (0, 0))],
            out_specs=pl.BlockSpec((2, TOK, 2 * QW), lambda i, p, s: (0, 0, 0)),
        ),
        out_shape=jax.ShapeDtypeStruct((2, TOK, 2 * QW), BF),
        cost_estimate=pl.CostEstimate(flops=0, bytes_accessed=3 << 20, transcendentals=0),
        compiler_params=pltpu.CompilerParams(vmem_limit_bytes=SMALL_LIMIT),
        name="place_q",
    )(*where, kept_own, kept_other, new)


def place_kv_kernel(pos, slot, kept_own, new_own, other, out_k, out_v):
    for core in range(2):

        @pl.when(core_of(pos) == core)
        def _():
            for slot_out, at, part, start in (
                (0, core, kept_own, 0),
                (0, 1 - core, other, 0),
                (1, core, new_own, 0),
                (1, 1 - core, other, KVW),
            ):
                for g in range(LOCAL_KV):
                    to = slice(at * KW + g * DH, at * KW + (g + 1) * DH)
                    mid = start + (2 * g + 1) * DH
                    out_k[slot_out, :, to] = part[:, mid - DH : mid]
                    out_v[slot_out, :, to] = part[:, mid : mid + DH]


def place_kv(where, kept_own, new, other):
    return pl.pallas_call(
        place_kv_kernel,
        grid_spec=pltpu.PrefetchScalarGridSpec(
            num_scalar_prefetch=2,
            grid=(1,),
            in_specs=[
                pl.BlockSpec((TOK, KVW), lambda i, p, s: (0, 0)),
                pl.BlockSpec((TOK, KVW), lambda i, p, s: (0, 2 * QW // KVW)),
                pl.BlockSpec((TOK, 2 * KVW), lambda i, p, s: (0, 0)),
            ],
            out_specs=[pl.BlockSpec((2, TOK, 2 * KW), lambda i, p, s: (0, 0, 0))] * 2,
        ),
        out_shape=[jax.ShapeDtypeStruct((2, TOK, 2 * KW), BF)] * 2,
        cost_estimate=pl.CostEstimate(flops=0, bytes_accessed=2 << 20, transcendentals=0),
        compiler_params=pltpu.CompilerParams(vmem_limit_bytes=SMALL_LIMIT),
        name="place_kv",
    )(*where, kept_own, new, other)


def core_swap(x):
    return lax.ppermute(x, "seq", [(i, i ^ 1) for i in range(2 * CHIPS)])


def up(x, d):
    pairs = [(2 * z + c, 2 * (z + d) + c) for z in range(CHIPS - d) for c in range(2)]
    return lax.ppermute(x, "seq", pairs)


def down(x, d):
    pairs = [(2 * (z + d) + c, 2 * z + c) for z in range(CHIPS - d) for c in range(2)]
    return lax.ppermute(x, "seq", pairs)


def trade(swap_mask, handed, sends):
    replicas = lax.axis_size("dp")

    def branch(mask, handed, sends):
        sums = [down(x, d + 1) for d, x in enumerate(sends)]
        return lax.ppermute(handed, "dp", [(r, r ^ mask) for r in range(replicas)]), sums

    branches = [functools.partial(branch, mask) for mask in range(1, replicas)]
    return lax.switch(swap_mask[0] - 1, branches, handed, sends)


def per_device(queries, key_rows, value_rows, cotangent, episodes, send_slot, swap_mask):
    tied = lax.optimization_barrier
    where = (lax.axis_index("seq").reshape(1).astype(jnp.int32), send_slot)
    got = core_swap(pack_kv(where, key_rows, value_rows, episodes))
    chunk_h, chunk_k = make_chunks(where, key_rows, value_rows, episodes, got)
    chunks_h = [chunk_h] + [up(chunk_h, d) for d in range(1, CHIPS)]
    *chunks_h, chunk_k, queries, cotangent = tied((*chunks_h, chunk_k, queries, cotangent))
    q_other = core_swap(pack_q(where, queries, cotangent))
    chunks_k = [chunk_k] + [up(chunk_k, d) for d in range(1, CHIPS)]

    gq_own, gq_other, *parts = attention(
        where, 0, queries, cotangent, q_other, chunks_h, chunks_h
    )
    sums = [parts[0]] + [down(parts[d], d) for d in range(1, CHIPS)]
    gq_got = core_swap(gq_other)
    *chunks_k, gq_own = tied((*chunks_k, gq_own))
    kept_own, kept_other, *parts = attention(
        where, 1, queries, cotangent, q_other, chunks_k, chunks_h
    )
    *sums, gq_own, gq_got, kept_own = tied((*sums, gq_own, gq_got, kept_own))
    new, sums = trade(swap_mask, hand_over(sums, gq_own, gq_got), parts[1:])
    kv_own, kv_other = keep([parts[0]] + sums, new)
    kept_other, kv_other = core_swap(kept_other), core_swap(kv_other)
    grad_queries = place_q(where, kept_own, kept_other, new)
    grad_keys, grad_values = place_kv(where, kv_own, new, kv_other)
    return grad_queries, grad_keys, grad_values


def solution(mesh):
    spec = P("dp", "seq", None)
    return jax.shard_map(
        per_device,
        mesh=mesh,
        in_specs=(spec, spec, spec, spec, P("dp", "seq"), P("dp"), P()),
        out_specs=(spec, spec, spec),
        check_vma=False,
    )
```

profile of v0, /device:TPU:1, one launch (start us, length us, event | category | flops | bytes accessed | tf_op | source)
XLA Modules:
  0.0 95.8 jit_solution(1997992255583041804)
XLA Ops:
  1.4 0.9 copy-done.3
  2.3 0.9 copy-done.4
  3.3 0.7 copy-done.5
  4.0 0.1 pack_kv.1
  4.1 1.5 %collective-permute-start.60 = (bf16[2,80,1024]{2,1,0:T(8,128)(2,1)S(1)}, bf16[2,80,1024]{2,1,0:T(8,128)(2,1)S(1)}, u32[]{:S(2)}, u32[]{:S(2)}) collective-permute-start(bf16[2,80,1024]{2,1,0:T(8,128)(2,1)S(1)} %pack_kv.1), channel_id=1, source_target_pairs={{0,1},{1,0},{2,3},{3,2},{4,5},{5,4},{6,7},{7,6},{8,9},{9,8},{10,11... | collective-permute-start | bytes 983048 | tf_op jit(solution)/shard_map/ppermute | solution.py:350
  5.6 1.3 %collective-permute-done.60.got = bf16[2,80,1024]{2,1,0:T(8,128)(2,1)S(1)} collective-permute-done((bf16[2,80,1024]{2,1,0:T(8,128)(2,1)S(1)}, bf16[2,80,1024]{2,1,0:T(8,128)(2,1)S(1)}, u32[]{:S(2)}, u32[]{:S(2)}) %collective-permute-start.60) | collective-permute-done | bytes 327712 | tf_op jit(solution)/shard_map/ppermute | solution.py:350
  6.8 0.1 make_chunks.1
  6.9 3.6 %collective-permute-start.61 = (bf16[144,1024]{1,0:T(8,128)(2,1)S(1)}, bf16[144,1024]{1,0:T(8,128)(2,1)S(1)}, u32[]{:S(2)}, u32[]{:S(2)}) collective-permute-start(bf16[144,1024]{1,0:T(8,128)(2,1)S(1)} %get-tuple-element.228.k0.i0), channel_id=1, source_target_pairs={{0,2},{1,3},{2,4},{3,5},{4,6},{5,7},{8,10},{9,11},{10,12},{11,13},... | collective-permute-start | bytes 884744 | tf_op jit(solution)/shard_map/ppermute | solution.py:355
  10.6 5.2 %collective-permute-start.62 = (bf16[144,1024]{1,0:T(8,128)(2,1)S(1)}, bf16[144,1024]{1,0:T(8,128)(2,1)S(1)}, u32[]{:S(2)}, u32[]{:S(2)}) collective-permute-start(bf16[144,1024]{1,0:T(8,128)(2,1)S(1)} %get-tuple-element.228.k0.i0), channel_id=1, source_target_pairs={{0,4},{1,5},{2,6},{3,7},{8,12},{9,13},{10,14},{11,15},{16,20},{17,... | collective-permute-start | bytes 884744 | tf_op jit(solution)/shard_map/ppermute | solution.py:355
  15.8 1.3 %collective-permute-start.63 = (bf16[144,1024]{1,0:T(8,128)(2,1)S(1)}, bf16[144,1024]{1,0:T(8,128)(2,1)S(1)}, u32[]{:S(2)}, u32[]{:S(2)}) collective-permute-start(bf16[144,1024]{1,0:T(8,128)(2,1)S(1)} %get-tuple-element.228.k0.i0), channel_id=1, source_target_pairs={{0,6},{1,7},{8,14},{9,15},{16,22},{17,23},{24,30},{25,31},{32,38},... | collective-permute-start | bytes 884744 | tf_op jit(solution)/shard_map/ppermute | solution.py:355
  17.1 0.0 collective-permute-done.61.k1.i1
  17.1 5.8 %collective-permute-done.62.k2.i2 = bf16[144,1024]{1,0:T(8,128)(2,1)S(1)} collective-permute-done((bf16[144,1024]{1,0:T(8,128)(2,1)S(1)}, bf16[144,1024]{1,0:T(8,128)(2,1)S(1)}, u32[]{:S(2)}, u32[]{:S(2)}) %collective-permute-start.62) | collective-permute-done | bytes 294944 | tf_op jit(solution)/shard_map/ppermute | solution.py:355
  22.9 4.4 %collective-permute-done.63.k3.i3 = bf16[144,1024]{1,0:T(8,128)(2,1)S(1)} collective-permute-done((bf16[144,1024]{1,0:T(8,128)(2,1)S(1)}, bf16[144,1024]{1,0:T(8,128)(2,1)S(1)}, u32[]{:S(2)}, u32[]{:S(2)}) %collective-permute-start.63) | collective-permute-done | bytes 294944 | tf_op jit(solution)/shard_map/ppermute | solution.py:355
  27.3 1.3 %copy-done.1 = bf16[2,64,5120]{2,1,0:T(8,128)(2,1)S(1)} copy-done((bf16[2,64,5120]{2,1,0:T(8,128)(2,1)S(1)}, bf16[2,64,5120]{2,1,0:T(8,128)(2,1)}, u32[]{:S(2)}) %copy-start.1) | copy-done | bytes 1310744
  28.6 0.3 pack_q.1
  28.9 0.6 collective-permute-start.64
  29.4 1.3 %collective-permute-start.68 = (bf16[128,1024]{1,0:T(8,128)(2,1)S(1)}, bf16[128,1024]{1,0:T(8,128)(2,1)S(1)}, u32[]{:S(2)}, u32[]{:S(2)}) collective-permute-start(bf16[128,1024]{1,0:T(8,128)(2,1)S(1)} %get-tuple-element.240.k0), channel_id=1, source_target_pairs={{0,2},{1,3},{2,4},{3,5},{4,6},{5,7},{8,10},{9,11},{10,12},{11,13},... | collective-permute-start | bytes 786440 | tf_op jit(solution)/shard_map/ppermute | solution.py:355
  30.7 7.1 %collective-permute-start.69 = (bf16[128,1024]{1,0:T(8,128)(2,1)S(1)}, bf16[128,1024]{1,0:T(8,128)(2,1)S(1)}, u32[]{:S(2)}, u32[]{:S(2)}) collective-permute-start(bf16[128,1024]{1,0:T(8,128)(2,1)S(1)} %get-tuple-element.240.k0), channel_id=1, source_target_pairs={{0,4},{1,5},{2,6},{3,7},{8,12},{9,13},{10,14},{11,15},{16,20},{17,... | collective-permute-start | bytes 786440 | tf_op jit(solution)/shard_map/ppermute | solution.py:355
  37.9 1.3 %collective-permute-start.70 = (bf16[128,1024]{1,0:T(8,128)(2,1)S(1)}, bf16[128,1024]{1,0:T(8,128)(2,1)S(1)}, u32[]{:S(2)}, u32[]{:S(2)}) collective-permute-start(bf16[128,1024]{1,0:T(8,128)(2,1)S(1)} %get-tuple-element.240.k0), channel_id=1, source_target_pairs={{0,6},{1,7},{8,14},{9,15},{16,22},{17,23},{24,30},{25,31},{32,38},... | collective-permute-start | bytes 786440 | tf_op jit(solution)/shard_map/ppermute | solution.py:355
  39.2 0.0 collective-permute-done.64.qx
  39.2 7.4 %attention.2 = (bf16[64,2560]{1,0:T(8,128)(2,1)S(1)}, bf16[64,2560]{1,0:T(8,128)(2,1)S(1)}, f32[128,1024]{1,0:T(8,128)S(1)}, bf16[128,1024]{1,0:T(8,128)(2,1)S(1...) custom-call(s32[1]{0:T(128)} %bitcast.pos, s32[1]{0:T(128)S(6)} %copy.70.slot, ...), custom_call_target="tpu_custom_call" | custom-call | flops 1677721600 | bytes 5242880 | tf_op jit(solution)/shard_map/attention/pallas_call | solution.py:203
  46.6 0.8 collective-permute-start.71
  47.4 1.3 %collective-permute-start.65 = (bf16[128,1024]{1,0:T(8,128)(2,1)S(1)}, bf16[128,1024]{1,0:T(8,128)(2,1)S(1)}, u32[]{:S(2)}, u32[]{:S(2)}) collective-permute-start(bf16[128,1024]{1,0:T(8,128)(2,1)S(1)} %get-tuple-element.233), channel_id=1, source_target_pairs={{2,0},{3,1},{4,2},{5,3},{6,4},{7,5},{10,8},{11,9},{12,10},{13,11},... | collective-permute-start | bytes 786440 | tf_op jit(solution)/shard_map/ppermute | solution.py:360
  48.7 0.0 collective-permute-done.68.k1
  48.7 1.3 %collective-permute-start.66 = (bf16[128,1024]{1,0:T(8,128)(2,1)S(1)}, bf16[128,1024]{1,0:T(8,128)(2,1)S(1)}, u32[]{:S(2)}, u32[]{:S(2)}) collective-permute-start(bf16[128,1024]{1,0:T(8,128)(2,1)S(1)} %get-tuple-element.234), channel_id=1, source_target_pairs={{4,0},{5,1},{6,2},{7,3},{12,8},{13,9},{14,10},{15,11},{20,16},{21,... | collective-permute-start | bytes 786440 | tf_op jit(solution)/shard_map/ppermute | solution.py:360
  50.0 0.0 collective-permute-done.69.k2
  50.0 1.3 %collective-permute-start.67 = (bf16[128,1024]{1,0:T(8,128)(2,1)S(1)}, bf16[128,1024]{1,0:T(8,128)(2,1)S(1)}, u32[]{:S(2)}, u32[]{:S(2)}) collective-permute-start(bf16[128,1024]{1,0:T(8,128)(2,1)S(1)} %get-tuple-element.235), channel_id=1, source_target_pairs={{6,0},{7,1},{14,8},{15,9},{22,16},{23,17},{30,24},{31,25},{38,32},... | collective-permute-start | bytes 786440 | tf_op jit(solution)/shard_map/ppermute | solution.py:360
  51.3 7.4 %attention.3 = (bf16[64,2560]{1,0:T(8,128)(2,1)S(1)}, bf16[64,2560]{1,0:T(8,128)(2,1)S(1)}, f32[128,1024]{1,0:T(8,128)S(1)}, bf16[128,1024]{1,0:T(8,128)(2,1)S(1...) custom-call(s32[1]{0:T(128)} %bitcast.pos, s32[1]{0:T(128)S(6)} %copy.70.slot, ...), custom_call_target="tpu_custom_call" | custom-call | flops 1677721600 | bytes 5242880 | tf_op jit(solution)/shard_map/attention/pallas_call | solution.py:203
  58.7 0.1 collective-permute-start.72
  59.5 0.0 collective-permute-done.65.r1
  59.5 0.6 collective-permute-done.66.r2
  60.0 5.9 %collective-permute-done.67.r3 = bf16[128,1024]{1,0:T(8,128)(2,1)S(1)} collective-permute-done((bf16[128,1024]{1,0:T(8,128)(2,1)S(1)}, bf16[128,1024]{1,0:T(8,128)(2,1)S(1)}, u32[]{:S(2)}, u32[]{:S(2)}) %collective-permute-start.67) | collective-permute-done | bytes 262176 | tf_op jit(solution)/shard_map/ppermute | solution.py:360
  66.0 0.0 collective-permute-done.71.gq_got
  66.0 0.2 hand_over.1
  66.1 23.0 %conditional.1 = (bf16[64,7168]{1,0:T(8,128)(2,1)}, bf16[128,1024]{1,0:T(8,128)(2,1)}, bf16[128,1024]{1,0:T(8,128)(2,1)}, bf16[128,1024]{1,0:T(8,128)(2,1)}) conditional(s32[]{:T(128)} %bitcast.1, (bf16[64,7168]{1,0:T(8,128)(2,1)S(1)}, bf16[128,1024]{1,0:T(8,128)(2,1)S(1)}, bf16[128,1024]{1,0:T(8,128)(2,1)S(1)}, ...), branch_computations={%region_0.0_spmd, %region_1.0_spmd, %region_2.0_spmd, %region_3.0_... | conditional | bytes 6815936 | solution.py:371
  66.2 2.8 %collective-permute-start.8 = (bf16[64,7168]{1,0:T(8,128)(2,1)S(1)}, bf16[64,7168]{1,0:T(8,128)(2,1)}, u32[]{:S(2)}, u32[]{:S(2)}) collective-permute-start(bf16[64,7168]{1,0:T(8,128)(2,1)S(1)} %get-tuple-element.128), channel_id=1, source_target_pairs={{0,24},{8,16},{16,8},{24,0},{32,56},{40,48},{48,40},{56,32},{64,88... | collective-permute-start | bytes 2752520 | tf_op jit(solution)/shard_map/cond/branch_2_fun/ppermute | solution.py:368
  69.0 1.3 %collective-permute-start.9 = (bf16[128,1024]{1,0:T(8,128)(2,1)S(1)}, bf16[128,1024]{1,0:T(8,128)(2,1)}, u32[]{:S(2)}, u32[]{:S(2)}) collective-permute-start(bf16[128,1024]{1,0:T(8,128)(2,1)S(1)} %get-tuple-element.129), channel_id=1, source_target_pairs={{2,0},{3,1},{4,2},{5,3},{6,4},{7,5},{10,8},{11,9},{12,10},{13,11},... | collective-permute-start | bytes 786440 | tf_op jit(solution)/shard_map/cond/branch_2_fun/ppermute | solution.py:360
  70.3 1.3 %collective-permute-start.10 = (bf16[128,1024]{1,0:T(8,128)(2,1)S(1)}, bf16[128,1024]{1,0:T(8,128)(2,1)}, u32[]{:S(2)}, u32[]{:S(2)}) collective-permute-start(bf16[128,1024]{1,0:T(8,128)(2,1)S(1)} %get-tuple-element.130), channel_id=1, source_target_pairs={{4,0},{5,1},{6,2},{7,3},{12,8},{13,9},{14,10},{15,11},{20,16},{21,... | collective-permute-start | bytes 786440 | tf_op jit(solution)/shard_map/cond/branch_2_fun/ppermute | solution.py:360
  71.6 1.3 %collective-permute-start.11 = (bf16[128,1024]{1,0:T(8,128)(2,1)S(1)}, bf16[128,1024]{1,0:T(8,128)(2,1)}, u32[]{:S(2)}, u32[]{:S(2)}) collective-permute-start(bf16[128,1024]{1,0:T(8,128)(2,1)S(1)} %get-tuple-element.131), channel_id=1, source_target_pairs={{6,0},{7,1},{14,8},{15,9},{22,16},{23,17},{30,24},{31,25},{38,32},... | collective-permute-start | bytes 786440 | tf_op jit(solution)/shard_map/cond/branch_2_fun/ppermute | solution.py:360
  72.9 5.2 %collective-permute-done.9 = bf16[128,1024]{1,0:T(8,128)(2,1)} collective-permute-done((bf16[128,1024]{1,0:T(8,128)(2,1)S(1)}, bf16[128,1024]{1,0:T(8,128)(2,1)}, u32[]{:S(2)}, u32[]{:S(2)}) %collective-permute-start.9) | collective-permute-done | bytes 262176 | tf_op jit(solution)/shard_map/cond/branch_2_fun/ppermute | solution.py:360
  78.1 2.8 %collective-permute-done.10 = bf16[128,1024]{1,0:T(8,128)(2,1)} collective-permute-done((bf16[128,1024]{1,0:T(8,128)(2,1)S(1)}, bf16[128,1024]{1,0:T(8,128)(2,1)}, u32[]{:S(2)}, u32[]{:S(2)}) %collective-permute-start.10) | collective-permute-done | bytes 262176 | tf_op jit(solution)/shard_map/cond/branch_2_fun/ppermute | solution.py:360
  80.9 6.8 %collective-permute-done.11 = bf16[128,1024]{1,0:T(8,128)(2,1)} collective-permute-done((bf16[128,1024]{1,0:T(8,128)(2,1)S(1)}, bf16[128,1024]{1,0:T(8,128)(2,1)}, u32[]{:S(2)}, u32[]{:S(2)}) %collective-permute-start.11) | collective-permute-done | bytes 262176 | tf_op jit(solution)/shard_map/cond/branch_2_fun/ppermute | solution.py:360
  87.6 1.5 %collective-permute-done.8 = bf16[64,7168]{1,0:T(8,128)(2,1)} collective-permute-done((bf16[64,7168]{1,0:T(8,128)(2,1)S(1)}, bf16[64,7168]{1,0:T(8,128)(2,1)}, u32[]{:S(2)}, u32[]{:S(2)}) %collective-permute-start.8) | collective-permute-done | bytes 917536 | tf_op jit(solution)/shard_map/cond/branch_2_fun/ppermute | solution.py:368
  89.2 1.3 %keep.1 = (bf16[64,1024]{1,0:T(8,128)(2,1)S(1)}, bf16[64,2048]{1,0:T(8,128)(2,1)S(1)}) custom-call(f32[128,1024]{1,0:T(8,128)S(1)} %get-tuple-element.257.p0, bf16[128,1024]{1,0:T(8,128)(2,1)} %get-tuple-element.258.r1, bf16[128,1024]{1,0:T(8,128)(2,1)} %get-tuple-element.259.r2, bf16[128,1024]{1,0:T(8,128)(2,1)} %get-tuple-element.260.r3, ...), custom_call_target="tpu_custom_call" | custom-call | bytes 2097152 | tf_op jit(solution)/shard_map/keep/pallas_call | solution.py:265
  90.4 1.3 %collective-permute-start.73 = (bf16[64,2048]{1,0:T(8,128)(2,1)S(1)}, bf16[64,2048]{1,0:T(8,128)(2,1)S(1)}, u32[]{:S(2)}, u32[]{:S(2)}) collective-permute-start(bf16[64,2048]{1,0:T(8,128)(2,1)S(1)} %get-tuple-element.262), channel_id=1, source_target_pairs={{0,1},{1,0},{2,3},{3,2},{4,5},{5,4},{6,7},{7,6},{8,9},{9,8},{10,11... | collective-permute-start | bytes 786440 | tf_op jit(solution)/shard_map/ppermute | solution.py:350
  91.7 2.2 %place_q.1 = bf16[2,64,5120]{2,1,0:T(8,128)(2,1)} custom-call(s32[1]{0:T(128)} %bitcast.pos, s32[1]{0:T(128)S(6)} %copy.70.slot, bf16[64,2560]{1,0:T(8,128)(2,1)S(1)} %get-tuple-element.245.kept_own, bf16[64,2560]{1,0:T(8,128)(2,1)S(1)} %collective-permute-done.72.kept_other, bf16[64,7168]{1,0:T(8,128)(2,1)} %get-tuple-element.256.new.new_own), custom_call_target="tpu_custom_call" | custom-call | bytes 3145728 | tf_op jit(solution)/shard_map/place_q/pallas_call | solution.py:295
  94.0 0.0 collective-permute-done.73.other
  94.0 1.8 %place_kv.1 = (bf16[2,64,1024]{2,1,0:T(8,128)(2,1)}, bf16[2,64,1024]{2,1,0:T(8,128)(2,1)}) custom-call(s32[1]{0:T(128)} %bitcast.pos, s32[1]{0:T(128)S(6)} %copy.70.slot, bf16[64,1024]{1,0:T(8,128)(2,1)S(1)} %get-tuple-element.261.kept_own, bf16[64,7168]{1,0:T(8,128)(2,1)} %get-tuple-element.256.new.new_own, bf16[64,2048]{1,0:T(8,128)(2,1)S(1)} %collective-permute-done.73.other), custom_call_target="tpu_custom_call" | custom-call | bytes 2097152 | tf_op jit(solution)/shard_map/place_kv/pallas_call | solution.py:330
  (10 shorter events, 0.0 us)
Async XLA Ops:
  0.6 26.7 %copy-start = (bf16[2,64,5120]{2,1,0:T(8,128)(2,1)S(1)}, bf16[2,64,5120]{2,1,0:T(8,128)(2,1)}, u32[]{:S(2)}) copy-start(bf16[2,64,5120]{2,1,0:T(8,128)(2,1)} %qo.1) | copy-start | bytes 3932164
  1.4 1.0 copy-start.3
  2.3 0.9 copy-start.4
  3.3 0.7 copy-start.5
  4.1 2.8 %collective-permute-start.60 = (bf16[2,80,1024]{2,1,0:T(8,128)(2,1)S(1)}, bf16[2,80,1024]{2,1,0:T(8,128)(2,1)S(1)}, u32[]{:S(2)}, u32[]{:S(2)}) collective-permute-start(bf16[2,80,1024]{2,1,0:T(8,128)(2,1)S(1)} %pack_kv.1), channel_id=1, source_target_pairs={{0,1},{1,0},{2,3},{3,2},{4,5},{5,4},{6,7},{7,6},{8,9},{9,8},{10,11... | collective-permute-start | bytes 983048 | tf_op jit(solution)/shard_map/ppermute | solution.py:350
  6.9 10.2 %collective-permute-start.61 = (bf16[144,1024]{1,0:T(8,128)(2,1)S(1)}, bf16[144,1024]{1,0:T(8,128)(2,1)S(1)}, u32[]{:S(2)}, u32[]{:S(2)}) collective-permute-start(bf16[144,1024]{1,0:T(8,128)(2,1)S(1)} %get-tuple-element.228.k0.i0), channel_id=1, source_target_pairs={{0,2},{1,3},{2,4},{3,5},{4,6},{5,7},{8,10},{9,11},{10,12},{11,13},... | collective-permute-start | bytes 884744 | tf_op jit(solution)/shard_map/ppermute | solution.py:355
  10.6 12.4 %collective-permute-start.62 = (bf16[144,1024]{1,0:T(8,128)(2,1)S(1)}, bf16[144,1024]{1,0:T(8,128)(2,1)S(1)}, u32[]{:S(2)}, u32[]{:S(2)}) collective-permute-start(bf16[144,1024]{1,0:T(8,128)(2,1)S(1)} %get-tuple-element.228.k0.i0), channel_id=1, source_target_pairs={{0,4},{1,5},{2,6},{3,7},{8,12},{9,13},{10,14},{11,15},{16,20},{17,... | collective-permute-start | bytes 884744 | tf_op jit(solution)/shard_map/ppermute | solution.py:355
  15.8 11.5 %collective-permute-start.63 = (bf16[144,1024]{1,0:T(8,128)(2,1)S(1)}, bf16[144,1024]{1,0:T(8,128)(2,1)S(1)}, u32[]{:S(2)}, u32[]{:S(2)}) collective-permute-start(bf16[144,1024]{1,0:T(8,128)(2,1)S(1)} %get-tuple-element.228.k0.i0), channel_id=1, source_target_pairs={{0,6},{1,7},{8,14},{9,15},{16,22},{17,23},{24,30},{25,31},{32,38},... | collective-permute-start | bytes 884744 | tf_op jit(solution)/shard_map/ppermute | solution.py:355
  27.3 1.3 %copy-start.1 = (bf16[2,64,5120]{2,1,0:T(8,128)(2,1)S(1)}, bf16[2,64,5120]{2,1,0:T(8,128)(2,1)}, u32[]{:S(2)}) copy-start(bf16[2,64,5120]{2,1,0:T(8,128)(2,1)} %co.1) | copy-start | bytes 3932164
  28.6 10.6 %copy-start.2 = (bf16[2,64,5120]{2,1,0:T(8,128)(2,1)S(1)}, bf16[2,64,5120]{2,1,0:T(8,128)(2,1)}, u32[]{:S(2)}) copy-start(bf16[2,64,5120]{2,1,0:T(8,128)(2,1)} %co.1) | copy-start | bytes 3932164
  28.9 10.3 %collective-permute-start.64 = (bf16[2,2,64,2560]{3,2,1,0:T(8,128)(2,1)S(1)}, bf16[2,2,64,2560]{3,2,1,0:T(8,128)(2,1)S(1)}, u32[]{:S(2)}, u32[]{:S(2)}) collective-permute-start(bf16[2,2,64,2560]{3,2,1,0:T(8,128)(2,1)S(1)} %pack_q.1), channel_id=1, source_target_pairs={{0,1},{1,0},{2,3},{3,2},{4,5},{5,4},{6,7},{7,6},{8,9},{9,8},{10,11... | collective-permute-start | bytes 3932168 | tf_op jit(solution)/shard_map/ppermute | solution.py:350
  29.4 19.2 %collective-permute-start.68 = (bf16[128,1024]{1,0:T(8,128)(2,1)S(1)}, bf16[128,1024]{1,0:T(8,128)(2,1)S(1)}, u32[]{:S(2)}, u32[]{:S(2)}) collective-permute-start(bf16[128,1024]{1,0:T(8,128)(2,1)S(1)} %get-tuple-element.240.k0), channel_id=1, source_target_pairs={{0,2},{1,3},{2,4},{3,5},{4,6},{5,7},{8,10},{9,11},{10,12},{11,13},... | collective-permute-start | bytes 786440 | tf_op jit(solution)/shard_map/ppermute | solution.py:355
  30.7 19.2 %collective-permute-start.69 = (bf16[128,1024]{1,0:T(8,128)(2,1)S(1)}, bf16[128,1024]{1,0:T(8,128)(2,1)S(1)}, u32[]{:S(2)}, u32[]{:S(2)}) collective-permute-start(bf16[128,1024]{1,0:T(8,128)(2,1)S(1)} %get-tuple-element.240.k0), channel_id=1, source_target_pairs={{0,4},{1,5},{2,6},{3,7},{8,12},{9,13},{10,14},{11,15},{16,20},{17,... | collective-permute-start | bytes 786440 | tf_op jit(solution)/shard_map/ppermute | solution.py:355
  37.9 13.4 %collective-permute-start.70 = (bf16[128,1024]{1,0:T(8,128)(2,1)S(1)}, bf16[128,1024]{1,0:T(8,128)(2,1)S(1)}, u32[]{:S(2)}, u32[]{:S(2)}) collective-permute-start(bf16[128,1024]{1,0:T(8,128)(2,1)S(1)} %get-tuple-element.240.k0), channel_id=1, source_target_pairs={{0,6},{1,7},{8,14},{9,15},{16,22},{17,23},{24,30},{25,31},{32,38},... | collective-permute-start | bytes 786440 | tf_op jit(solution)/shard_map/ppermute | solution.py:355
  46.6 19.4 %collective-permute-start.71 = (bf16[64,2560]{1,0:T(8,128)(2,1)S(1)}, bf16[64,2560]{1,0:T(8,128)(2,1)S(1)}, u32[]{:S(2)}, u32[]{:S(2)}) collective-permute-start(bf16[64,2560]{1,0:T(8,128)(2,1)S(1)} %get-tuple-element.239), channel_id=1, source_target_pairs={{0,1},{1,0},{2,3},{3,2},{4,5},{5,4},{6,7},{7,6},{8,9},{9,8},{10,11... | collective-permute-start | bytes 983048 | tf_op jit(solution)/shard_map/ppermute | solution.py:350
  47.4 12.1 %collective-permute-start.65 = (bf16[128,1024]{1,0:T(8,128)(2,1)S(1)}, bf16[128,1024]{1,0:T(8,128)(2,1)S(1)}, u32[]{:S(2)}, u32[]{:S(2)}) collective-permute-start(bf16[128,1024]{1,0:T(8,128)(2,1)S(1)} %get-tuple-element.233), channel_id=1, source_target_pairs={{2,0},{3,1},{4,2},{5,3},{6,4},{7,5},{10,8},{11,9},{12,10},{13,11},... | collective-permute-start | bytes 786440 | tf_op jit(solution)/shard_map/ppermute | solution.py:360
  48.7 11.4 %collective-permute-start.66 = (bf16[128,1024]{1,0:T(8,128)(2,1)S(1)}, bf16[128,1024]{1,0:T(8,128)(2,1)S(1)}, u32[]{:S(2)}, u32[]{:S(2)}) collective-permute-start(bf16[128,1024]{1,0:T(8,128)(2,1)S(1)} %get-tuple-element.234), channel_id=1, source_target_pairs={{4,0},{5,1},{6,2},{7,3},{12,8},{13,9},{14,10},{15,11},{20,16},{21,... | collective-permute-start | bytes 786440 | tf_op jit(solution)/shard_map/ppermute | solution.py:360
  50.0 16.0 %collective-permute-start.67 = (bf16[128,1024]{1,0:T(8,128)(2,1)S(1)}, bf16[128,1024]{1,0:T(8,128)(2,1)S(1)}, u32[]{:S(2)}, u32[]{:S(2)}) collective-permute-start(bf16[128,1024]{1,0:T(8,128)(2,1)S(1)} %get-tuple-element.235), channel_id=1, source_target_pairs={{6,0},{7,1},{14,8},{15,9},{22,16},{23,17},{30,24},{31,25},{38,32},... | collective-permute-start | bytes 786440 | tf_op jit(solution)/shard_map/ppermute | solution.py:360
  58.7 33.0 %collective-permute-start.72 = (bf16[64,2560]{1,0:T(8,128)(2,1)S(1)}, bf16[64,2560]{1,0:T(8,128)(2,1)S(1)}, u32[]{:S(2)}, u32[]{:S(2)}) collective-permute-start(bf16[64,2560]{1,0:T(8,128)(2,1)S(1)} %get-tuple-element.246), channel_id=1, source_target_pairs={{0,1},{1,0},{2,3},{3,2},{4,5},{5,4},{6,7},{7,6},{8,9},{9,8},{10,11... | collective-permute-start | bytes 983048 | tf_op jit(solution)/shard_map/ppermute | solution.py:350
  66.2 23.0 %collective-permute-start.8 = (bf16[64,7168]{1,0:T(8,128)(2,1)S(1)}, bf16[64,7168]{1,0:T(8,128)(2,1)}, u32[]{:S(2)}, u32[]{:S(2)}) collective-permute-start(bf16[64,7168]{1,0:T(8,128)(2,1)S(1)} %get-tuple-element.128), channel_id=1, source_target_pairs={{0,24},{8,16},{16,8},{24,0},{32,56},{40,48},{48,40},{56,32},{64,88... | collective-permute-start | bytes 2752520 | tf_op jit(solution)/shard_map/cond/branch_2_fun/ppermute | solution.py:368
  69.0 9.1 %collective-permute-start.9 = (bf16[128,1024]{1,0:T(8,128)(2,1)S(1)}, bf16[128,1024]{1,0:T(8,128)(2,1)}, u32[]{:S(2)}, u32[]{:S(2)}) collective-permute-start(bf16[128,1024]{1,0:T(8,128)(2,1)S(1)} %get-tuple-element.129), channel_id=1, source_target_pairs={{2,0},{3,1},{4,2},{5,3},{6,4},{7,5},{10,8},{11,9},{12,10},{13,11},... | collective-permute-start | bytes 786440 | tf_op jit(solution)/shard_map/cond/branch_2_fun/ppermute | solution.py:360
  70.3 10.6 %collective-permute-start.10 = (bf16[128,1024]{1,0:T(8,128)(2,1)S(1)}, bf16[128,1024]{1,0:T(8,128)(2,1)}, u32[]{:S(2)}, u32[]{:S(2)}) collective-permute-start(bf16[128,1024]{1,0:T(8,128)(2,1)S(1)} %get-tuple-element.130), channel_id=1, source_target_pairs={{4,0},{5,1},{6,2},{7,3},{12,8},{13,9},{14,10},{15,11},{20,16},{21,... | collective-permute-start | bytes 786440 | tf_op jit(solution)/shard_map/cond/branch_2_fun/ppermute | solution.py:360
  71.6 16.0 %collective-permute-start.11 = (bf16[128,1024]{1,0:T(8,128)(2,1)S(1)}, bf16[128,1024]{1,0:T(8,128)(2,1)}, u32[]{:S(2)}, u32[]{:S(2)}) collective-permute-start(bf16[128,1024]{1,0:T(8,128)(2,1)S(1)} %get-tuple-element.131), channel_id=1, source_target_pairs={{6,0},{7,1},{14,8},{15,9},{22,16},{23,17},{30,24},{31,25},{38,32},... | collective-permute-start | bytes 786440 | tf_op jit(solution)/shard_map/cond/branch_2_fun/ppermute | solution.py:360
  90.4 3.5 %collective-permute-start.73 = (bf16[64,2048]{1,0:T(8,128)(2,1)S(1)}, bf16[64,2048]{1,0:T(8,128)(2,1)S(1)}, u32[]{:S(2)}, u32[]{:S(2)}) collective-permute-start(bf16[64,2048]{1,0:T(8,128)(2,1)S(1)} %get-tuple-element.262), channel_id=1, source_target_pairs={{0,1},{1,0},{2,3},{3,2},{4,5},{5,4},{6,7},{7,6},{8,9},{9,8},{10,11... | collective-permute-start | bytes 786440 | tf_op jit(solution)/shard_map/ppermute | solution.py:350
where the time goes:
time: 97.6 us; the launch traced here: 95.8 us
  starting transfers between devices  34.7 us (36%)
  waiting for transfers between devices  34.2 us (35%)
  Pallas kernels  20.6 us (21%)
  local copies, waits for them, and re-layouts  3.9 us (4%)
  between operations  2.24 us (2%)
    ppermute x6, waiting for transfers between devices, down(): return lax.ppermute(x, 'seq', pairs)  21.2 us
    ppermute x6, starting transfers between devices, up(): return lax.ppermute(x, 'seq', pairs)  19.9 us
    pallas_call x2, Pallas kernels, attention(): pl.pallas_call(attention_kernel, grid_spec=pltpu.PrefetchScalarGridSpec(n...  14.8 us
    ppermute x6, waiting for transfers between devices, up(): return lax.ppermute(x, 'seq', pairs)  10.2 us
    ppermute x6, starting transfers between devices, down(): return lax.ppermute(x, 'seq', pairs)  7.73 us
    ppermute x5, starting transfers between devices, core_swap(): return lax.ppermute(x, 'seq', [(i, i ^ 1) for i in range(2 * CHIPS)])  4.27 us
    unnamed x12, local copies, waits for them, and re-layouts  3.9 us
    ppermute x1, starting transfers between devices, branch(): lax.ppermute(handed, 'dp', [(r, r ^ mask) for r in range(replicas)])  2.82 us
  transfers between devices with their start and end apart: 18, of which 9 were waited for; matrix products, arithmetic and copies ran while one was open for 0% of the time, Pallas kernels for 19%

commit v1 on v0

--- a/solution.py
+++ b/solution.py
@@ -350,21 +350,16 @@
     return lax.ppermute(x, "seq", [(i, i ^ 1) for i in range(2 * CHIPS)])
 
 
-def up(x, d):
-    pairs = [(2 * z + c, 2 * (z + d) + c) for z in range(CHIPS - d) for c in range(2)]
-    return lax.ppermute(x, "seq", pairs)
-
-
-def down(x, d):
-    pairs = [(2 * (z + d) + c, 2 * z + c) for z in range(CHIPS - d) for c in range(2)]
-    return lax.ppermute(x, "seq", pairs)
+def ring(x, d):
+    n = 2 * CHIPS
+    return lax.ppermute(x, "seq", [(i, (i + 2 * d) % n) for i in range(n)])
 
 
 def trade(swap_mask, handed, sends):
     replicas = lax.axis_size("dp")
 
     def branch(mask, handed, sends):
-        sums = [down(x, d + 1) for d, x in enumerate(sends)]
+        sums = [ring(x, -d - 1) for d, x in enumerate(sends)]
         return lax.ppermute(handed, "dp", [(r, r ^ mask) for r in range(replicas)]), sums
 
     branches = [functools.partial(branch, mask) for mask in range(1, replicas)]
@@ -376,15 +371,15 @@
     where = (lax.axis_index("seq").reshape(1).astype(jnp.int32), send_slot)
     got = core_swap(pack_kv(where, key_rows, value_rows, episodes))
     chunk_h, chunk_k = make_chunks(where, key_rows, value_rows, episodes, got)
-    chunks_h = [chunk_h] + [up(chunk_h, d) for d in range(1, CHIPS)]
+    chunks_h = [chunk_h] + [ring(chunk_h, d) for d in range(1, CHIPS)]
     *chunks_h, chunk_k, queries, cotangent = tied((*chunks_h, chunk_k, queries, cotangent))
     q_other = core_swap(pack_q(where, queries, cotangent))
-    chunks_k = [chunk_k] + [up(chunk_k, d) for d in range(1, CHIPS)]
+    chunks_k = [chunk_k] + [ring(chunk_k, d) for d in range(1, CHIPS)]
 
     gq_own, gq_other, *parts = attention(
         where, 0, queries, cotangent, q_other, chunks_h, chunks_h
     )
-    sums = [parts[0]] + [down(parts[d], d) for d in range(1, CHIPS)]
+    sums = [parts[0]] + [ring(parts[d], -d) for d in range(1, CHIPS)]
     gq_got = core_swap(gq_other)
     *chunks_k, gq_own = tied((*chunks_k, gq_own))
     kept_own, kept_other, *parts = attention(

time: 97.6 us -> 86.9 us (0.89); the launches traced: 95.8 us -> 86.1 us
  starting transfers between devices: 34.7 us -> 24.4 us
    ppermute x12, starting transfers between devices: 27.6 us -> 14.6 us  [ring(): return lax.ppermute(x, 'seq', [(i, (i + 2 * d) % n) for i in range(n)])]
    ppermute x5, starting transfers between devices: 4.27 us -> 6.96 us  [core_swap(): return lax.ppermute(x, 'seq', [(i, i ^ 1) for i in range(2 * CHIPS)])]
    ppermute x1, waiting for transfers between devices: 1.54 us -> 3.97 us  [branch(): lax.ppermute(handed, 'dp', [(r, r ^ mask) for r in range(replicas)])]
    ppermute x12, waiting for transfers between devices: 31.4 us -> 29.6 us  [ring(): return lax.ppermute(x, 'seq', [(i, (i + 2 * d) % n) for i in range(n)])]
  transfers between devices with their start and end apart: 18 -> 18, of which waited for: 9 -> 9; matrix products, arithmetic and copies ran while one was open for 0% -> 0% of each run, Pallas kernels for 19% -> 21%
where the time goes in v1:
time: 86.9 us; the launch traced here: 86.1 us
  waiting for transfers between devices  34.9 us (40%)
  starting transfers between devices  24.4 us (28%)
  Pallas kernels  20.5 us (24%)
  local copies, waits for them, and re-layouts  3.89 us (4%)
  between operations  2.14 us (2%)
    ppermute x12, waiting for transfers between devices, ring(): return lax.ppermute(x, 'seq', [(i, (i + 2 * d) % n) for i in range(n)])  29.6 us
    pallas_call x2, Pallas kernels, attention(): pl.pallas_call(attention_kernel, grid_spec=pltpu.PrefetchScalarGridSpec(n...  14.7 us
    ppermute x12, starting transfers between devices, ring(): return lax.ppermute(x, 'seq', [(i, (i + 2 * d) % n) for i in range(n)])  14.6 us
    ppermute x5, starting transfers between devices, core_swap(): return lax.ppermute(x, 'seq', [(i, i ^ 1) for i in range(2 * CHIPS)])  6.96 us
    ppermute x1, waiting for transfers between devices, branch(): lax.ppermute(handed, 'dp', [(r, r ^ mask) for r in range(replicas)])  3.97 us
    unnamed x12, local copies, waits for them, and re-layouts  3.89 us
    ppermute x1, starting transfers between devices, branch(): lax.ppermute(handed, 'dp', [(r, r ^ mask) for r in range(replicas)])  2.82 us
    pallas_call x1, Pallas kernels, place_q(): pl.pallas_call(place_q_kernel, grid_spec=pltpu.PrefetchScalarGridSpec(num...  2.23 us
  transfers between devices with their start and end apart: 18, of which 9 were waited for; matrix products, arithmetic and copies ran while one was open for 0% of the time, Pallas kernels for 21%

profile of v1, /device:TPU:1, one launch (start us, length us, event | category | flops | bytes accessed | tf_op | source)
XLA Modules:
  0.0 86.1 jit_solution(9444997020197220073)
XLA Ops:
  1.4 0.9 %copy-done.3 = bf16[2,64,1024]{2,1,0:T(8,128)(2,1)S(1)} copy-done((bf16[2,64,1024]{2,1,0:T(8,128)(2,1)S(1)}, bf16[2,64,1024]{2,1,0:T(8,128)(2,1)}, u32[]{:S(2)}) %copy-start.3) | copy-done | bytes 262168
  2.3 0.9 %copy-done.4 = bf16[2,64,1024]{2,1,0:T(8,128)(2,1)S(1)} copy-done((bf16[2,64,1024]{2,1,0:T(8,128)(2,1)S(1)}, bf16[2,64,1024]{2,1,0:T(8,128)(2,1)}, u32[]{:S(2)}) %copy-start.4) | copy-done | bytes 262168
  3.3 0.7 copy-done.5
  4.0 0.1 pack_kv.1
  4.1 1.5 %collective-permute-start.60 = (bf16[2,80,1024]{2,1,0:T(8,128)(2,1)S(1)}, bf16[2,80,1024]{2,1,0:T(8,128)(2,1)S(1)}, u32[]{:S(2)}, u32[]{:S(2)}) collective-permute-start(bf16[2,80,1024]{2,1,0:T(8,128)(2,1)S(1)} %pack_kv.1), channel_id=1, source_target_pairs={{0,1},{1,0},{2,3},{3,2},{4,5},{5,4},{6,7},{7,6},{8,9},{9,8},{10,11... | collective-permute-start | bytes 983048 | tf_op jit(solution)/shard_map/ppermute | solution.py:350
  5.6 1.3 %collective-permute-done.60.got = bf16[2,80,1024]{2,1,0:T(8,128)(2,1)S(1)} collective-permute-done((bf16[2,80,1024]{2,1,0:T(8,128)(2,1)S(1)}, bf16[2,80,1024]{2,1,0:T(8,128)(2,1)S(1)}, u32[]{:S(2)}, u32[]{:S(2)}) %collective-permute-start.60) | collective-permute-done | bytes 327712 | tf_op jit(solution)/shard_map/ppermute | solution.py:350
  6.8 0.1 make_chunks.1
  6.9 1.8 %collective-permute-start.61 = (bf16[144,1024]{1,0:T(8,128)(2,1)S(1)}, bf16[144,1024]{1,0:T(8,128)(2,1)S(1)}, u32[]{:S(2)}, u32[]{:S(2)}) collective-permute-start(bf16[144,1024]{1,0:T(8,128)(2,1)S(1)} %get-tuple-element.228.k0.i0), channel_id=1, source_target_pairs={{0,2},{1,3},{2,4},{3,5},{4,6},{5,7},{6,0},{7,1},{8,10},{9,11},{10,... | collective-permute-start | bytes 884744 | tf_op jit(solution)/shard_map/ppermute | solution.py:355
  8.7 3.3 %collective-permute-start.62 = (bf16[144,1024]{1,0:T(8,128)(2,1)S(1)}, bf16[144,1024]{1,0:T(8,128)(2,1)S(1)}, u32[]{:S(2)}, u32[]{:S(2)}) collective-permute-start(bf16[144,1024]{1,0:T(8,128)(2,1)S(1)} %get-tuple-element.228.k0.i0), channel_id=1, source_target_pairs={{0,4},{1,5},{2,6},{3,7},{4,0},{5,1},{6,2},{7,3},{8,12},{9,13},{10,... | collective-permute-start | bytes 884744 | tf_op jit(solution)/shard_map/ppermute | solution.py:355
  12.0 0.7 collective-permute-start.63
  12.7 5.2 %collective-permute-done.61.k1.i1 = bf16[144,1024]{1,0:T(8,128)(2,1)S(1)} collective-permute-done((bf16[144,1024]{1,0:T(8,128)(2,1)S(1)}, bf16[144,1024]{1,0:T(8,128)(2,1)S(1)}, u32[]{:S(2)}, u32[]{:S(2)}) %collective-permute-start.61) | collective-permute-done | bytes 294944 | tf_op jit(solution)/shard_map/ppermute | solution.py:355
  17.9 7.2 %collective-permute-done.62.k2.i2 = bf16[144,1024]{1,0:T(8,128)(2,1)S(1)} collective-permute-done((bf16[144,1024]{1,0:T(8,128)(2,1)S(1)}, bf16[144,1024]{1,0:T(8,128)(2,1)S(1)}, u32[]{:S(2)}, u32[]{:S(2)}) %collective-permute-start.62) | collective-permute-done | bytes 294944 | tf_op jit(solution)/shard_map/ppermute | solution.py:355
  25.1 0.0 collective-permute-done.63.k3.i3
  25.1 1.3 %copy-done.1 = bf16[2,64,5120]{2,1,0:T(8,128)(2,1)S(1)} copy-done((bf16[2,64,5120]{2,1,0:T(8,128)(2,1)S(1)}, bf16[2,64,5120]{2,1,0:T(8,128)(2,1)}, u32[]{:S(2)}) %copy-start.1) | copy-done | bytes 1310744
  26.4 0.3 pack_q.1
  26.7 1.3 %collective-permute-start.64 = (bf16[2,2,64,2560]{3,2,1,0:T(8,128)(2,1)S(1)}, bf16[2,2,64,2560]{3,2,1,0:T(8,128)(2,1)S(1)}, u32[]{:S(2)}, u32[]{:S(2)}) collective-permute-start(bf16[2,2,64,2560]{3,2,1,0:T(8,128)(2,1)S(1)} %pack_q.1), channel_id=1, source_target_pairs={{0,1},{1,0},{2,3},{3,2},{4,5},{5,4},{6,7},{7,6},{8,9},{9,8},{10,11... | collective-permute-start | bytes 3932168 | tf_op jit(solution)/shard_map/ppermute | solution.py:350
  27.9 1.0 %collective-permute-start.68 = (bf16[128,1024]{1,0:T(8,128)(2,1)S(1)}, bf16[128,1024]{1,0:T(8,128)(2,1)S(1)}, u32[]{:S(2)}, u32[]{:S(2)}) collective-permute-start(bf16[128,1024]{1,0:T(8,128)(2,1)S(1)} %get-tuple-element.240.k0), channel_id=1, source_target_pairs={{0,2},{1,3},{2,4},{3,5},{4,6},{5,7},{6,0},{7,1},{8,10},{9,11},{10,... | collective-permute-start | bytes 786440 | tf_op jit(solution)/shard_map/ppermute | solution.py:355
  28.9 2.1 %collective-permute-start.69 = (bf16[128,1024]{1,0:T(8,128)(2,1)S(1)}, bf16[128,1024]{1,0:T(8,128)(2,1)S(1)}, u32[]{:S(2)}, u32[]{:S(2)}) collective-permute-start(bf16[128,1024]{1,0:T(8,128)(2,1)S(1)} %get-tuple-element.240.k0), channel_id=1, source_target_pairs={{0,4},{1,5},{2,6},{3,7},{4,0},{5,1},{6,2},{7,3},{8,12},{9,13},{10,... | collective-permute-start | bytes 786440 | tf_op jit(solution)/shard_map/ppermute | solution.py:355
  31.0 1.0 %collective-permute-start.70 = (bf16[128,1024]{1,0:T(8,128)(2,1)S(1)}, bf16[128,1024]{1,0:T(8,128)(2,1)S(1)}, u32[]{:S(2)}, u32[]{:S(2)}) collective-permute-start(bf16[128,1024]{1,0:T(8,128)(2,1)S(1)} %get-tuple-element.240.k0), channel_id=1, source_target_pairs={{0,6},{1,7},{2,0},{3,1},{4,2},{5,3},{6,4},{7,5},{8,14},{9,15},{10,... | collective-permute-start | bytes 786440 | tf_op jit(solution)/shard_map/ppermute | solution.py:355
  32.0 0.0 collective-permute-done.64.qx
  32.0 7.3 %attention.2 = (bf16[64,2560]{1,0:T(8,128)(2,1)S(1)}, bf16[64,2560]{1,0:T(8,128)(2,1)S(1)}, f32[128,1024]{1,0:T(8,128)S(1)}, bf16[128,1024]{1,0:T(8,128)(2,1)S(1...) custom-call(s32[1]{0:T(128)} %bitcast.pos, s32[1]{0:T(128)S(6)} %copy.70.slot, ...), custom_call_target="tpu_custom_call" | custom-call | flops 1677721600 | bytes 5242880 | tf_op jit(solution)/shard_map/attention/pallas_call | solution.py:203
  39.3 1.0 %collective-permute-start.71 = (bf16[64,2560]{1,0:T(8,128)(2,1)S(1)}, bf16[64,2560]{1,0:T(8,128)(2,1)S(1)}, u32[]{:S(2)}, u32[]{:S(2)}) collective-permute-start(bf16[64,2560]{1,0:T(8,128)(2,1)S(1)} %get-tuple-element.239), channel_id=1, source_target_pairs={{0,1},{1,0},{2,3},{3,2},{4,5},{5,4},{6,7},{7,6},{8,9},{9,8},{10,11... | collective-permute-start | bytes 983048 | tf_op jit(solution)/shard_map/ppermute | solution.py:350
  40.3 0.2 collective-permute-start.65
  40.5 0.0 collective-permute-done.68.k1
  40.5 2.1 %collective-permute-start.66 = (bf16[128,1024]{1,0:T(8,128)(2,1)S(1)}, bf16[128,1024]{1,0:T(8,128)(2,1)S(1)}, u32[]{:S(2)}, u32[]{:S(2)}) collective-permute-start(bf16[128,1024]{1,0:T(8,128)(2,1)S(1)} %get-tuple-element.234), channel_id=1, source_target_pairs={{0,4},{1,5},{2,6},{3,7},{4,0},{5,1},{6,2},{7,3},{8,12},{9,13},{10,... | collective-permute-start | bytes 786440 | tf_op jit(solution)/shard_map/ppermute | solution.py:355
  42.6 0.4 collective-permute-done.69.k2
  43.0 0.0 collective-permute-start.67
  43.0 0.0 collective-permute-done.70.k3
  43.0 7.3 %attention.3 = (bf16[64,2560]{1,0:T(8,128)(2,1)S(1)}, bf16[64,2560]{1,0:T(8,128)(2,1)S(1)}, f32[128,1024]{1,0:T(8,128)S(1)}, bf16[128,1024]{1,0:T(8,128)(2,1)S(1...) custom-call(s32[1]{0:T(128)} %bitcast.pos, s32[1]{0:T(128)S(6)} %copy.70.slot, ...), custom_call_target="tpu_custom_call" | custom-call | flops 1677721600 | bytes 5242880 | tf_op jit(solution)/shard_map/attention/pallas_call | solution.py:203
  50.4 1.8 %collective-permute-start.72 = (bf16[64,2560]{1,0:T(8,128)(2,1)S(1)}, bf16[64,2560]{1,0:T(8,128)(2,1)S(1)}, u32[]{:S(2)}, u32[]{:S(2)}) collective-permute-start(bf16[64,2560]{1,0:T(8,128)(2,1)S(1)} %get-tuple-element.246), channel_id=1, source_target_pairs={{0,1},{1,0},{2,3},{3,2},{4,5},{5,4},{6,7},{7,6},{8,9},{9,8},{10,11... | collective-permute-start | bytes 983048 | tf_op jit(solution)/shard_map/ppermute | solution.py:350
  52.8 0.0 collective-permute-done.65.r1
  52.8 0.0 collective-permute-done.66.r2
  52.8 3.0 %collective-permute-done.67.r3 = bf16[128,1024]{1,0:T(8,128)(2,1)S(1)} collective-permute-done((bf16[128,1024]{1,0:T(8,128)(2,1)S(1)}, bf16[128,1024]{1,0:T(8,128)(2,1)S(1)}, u32[]{:S(2)}, u32[]{:S(2)}) %collective-permute-start.67) | collective-permute-done | bytes 262176 | tf_op jit(solution)/shard_map/ppermute | solution.py:355
  55.9 0.2 hand_over.1
  56.0 23.4 %conditional.1 = (bf16[64,7168]{1,0:T(8,128)(2,1)}, bf16[128,1024]{1,0:T(8,128)(2,1)}, bf16[128,1024]{1,0:T(8,128)(2,1)}, bf16[128,1024]{1,0:T(8,128)(2,1)}) conditional(s32[]{:T(128)} %bitcast.1, (bf16[64,7168]{1,0:T(8,128)(2,1)S(1)}, bf16[128,1024]{1,0:T(8,128)(2,1)S(1)}, bf16[128,1024]{1,0:T(8,128)(2,1)S(1)}, ...), branch_computations={%region_0.0_spmd, %region_1.0_spmd, %region_2.0_spmd, %region_3.0_... | conditional | bytes 6815936 | solution.py:366
  56.3 2.8 %collective-permute-start.28 = (bf16[64,7168]{1,0:T(8,128)(2,1)S(1)}, bf16[64,7168]{1,0:T(8,128)(2,1)}, u32[]{:S(2)}, u32[]{:S(2)}) collective-permute-start(bf16[64,7168]{1,0:T(8,128)(2,1)S(1)} %get-tuple-element.148), channel_id=1, source_target_pairs={{0,64},{8,72},{16,80},{24,88},{32,96},{40,104},{48,112},{56,120},{... | collective-permute-start | bytes 2752520 | tf_op jit(solution)/shard_map/cond/branch_7_fun/ppermute | solution.py:363
  59.1 0.9 %collective-permute-start.29 = (bf16[128,1024]{1,0:T(8,128)(2,1)S(1)}, bf16[128,1024]{1,0:T(8,128)(2,1)}, u32[]{:S(2)}, u32[]{:S(2)}) collective-permute-start(bf16[128,1024]{1,0:T(8,128)(2,1)S(1)} %get-tuple-element.149), channel_id=1, source_target_pairs={{0,6},{1,7},{2,0},{3,1},{4,2},{5,3},{6,4},{7,5},{8,14},{9,15},{10,... | collective-permute-start | bytes 786440 | tf_op jit(solution)/shard_map/cond/branch_7_fun/ppermute | solution.py:355
  60.0 0.9 %collective-permute-start.30 = (bf16[128,1024]{1,0:T(8,128)(2,1)S(1)}, bf16[128,1024]{1,0:T(8,128)(2,1)}, u32[]{:S(2)}, u32[]{:S(2)}) collective-permute-start(bf16[128,1024]{1,0:T(8,128)(2,1)S(1)} %get-tuple-element.150), channel_id=1, source_target_pairs={{0,4},{1,5},{2,6},{3,7},{4,0},{5,1},{6,2},{7,3},{8,12},{9,13},{10,... | collective-permute-start | bytes 786440 | tf_op jit(solution)/shard_map/cond/branch_7_fun/ppermute | solution.py:355
  60.9 0.7 collective-permute-start.31
  61.6 4.7 %collective-permute-done.29 = bf16[128,1024]{1,0:T(8,128)(2,1)} collective-permute-done((bf16[128,1024]{1,0:T(8,128)(2,1)S(1)}, bf16[128,1024]{1,0:T(8,128)(2,1)}, u32[]{:S(2)}, u32[]{:S(2)}) %collective-permute-start.29) | collective-permute-done | bytes 262176 | tf_op jit(solution)/shard_map/cond/branch_7_fun/ppermute | solution.py:355
  66.3 1.6 %collective-permute-done.30 = bf16[128,1024]{1,0:T(8,128)(2,1)} collective-permute-done((bf16[128,1024]{1,0:T(8,128)(2,1)S(1)}, bf16[128,1024]{1,0:T(8,128)(2,1)}, u32[]{:S(2)}, u32[]{:S(2)}) %collective-permute-start.30) | collective-permute-done | bytes 262176 | tf_op jit(solution)/shard_map/cond/branch_7_fun/ppermute | solution.py:355
  67.9 7.6 %collective-permute-done.31 = bf16[128,1024]{1,0:T(8,128)(2,1)} collective-permute-done((bf16[128,1024]{1,0:T(8,128)(2,1)S(1)}, bf16[128,1024]{1,0:T(8,128)(2,1)}, u32[]{:S(2)}, u32[]{:S(2)}) %collective-permute-start.31) | collective-permute-done | bytes 262176 | tf_op jit(solution)/shard_map/cond/branch_7_fun/ppermute | solution.py:355
  75.4 4.0 %collective-permute-done.28 = bf16[64,7168]{1,0:T(8,128)(2,1)} collective-permute-done((bf16[64,7168]{1,0:T(8,128)(2,1)S(1)}, bf16[64,7168]{1,0:T(8,128)(2,1)}, u32[]{:S(2)}, u32[]{:S(2)}) %collective-permute-start.28) | collective-permute-done | bytes 917536 | tf_op jit(solution)/shard_map/cond/branch_7_fun/ppermute | solution.py:363
  79.4 1.3 %keep.1 = (bf16[64,1024]{1,0:T(8,128)(2,1)S(1)}, bf16[64,2048]{1,0:T(8,128)(2,1)S(1)}) custom-call(f32[128,1024]{1,0:T(8,128)S(1)} %get-tuple-element.257.p0, bf16[128,1024]{1,0:T(8,128)(2,1)} %get-tuple-element.258.r1, bf16[128,1024]{1,0:T(8,128)(2,1)} %get-tuple-element.259.r2, bf16[128,1024]{1,0:T(8,128)(2,1)} %get-tuple-element.260.r3, ...), custom_call_target="tpu_custom_call" | custom-call | bytes 2097152 | tf_op jit(solution)/shard_map/keep/pallas_call | solution.py:265
  80.7 1.4 %collective-permute-start.73 = (bf16[64,2048]{1,0:T(8,128)(2,1)S(1)}, bf16[64,2048]{1,0:T(8,128)(2,1)S(1)}, u32[]{:S(2)}, u32[]{:S(2)}) collective-permute-start(bf16[64,2048]{1,0:T(8,128)(2,1)S(1)} %get-tuple-element.262), channel_id=1, source_target_pairs={{0,1},{1,0},{2,3},{3,2},{4,5},{5,4},{6,7},{7,6},{8,9},{9,8},{10,11... | collective-permute-start | bytes 786440 | tf_op jit(solution)/shard_map/ppermute | solution.py:350
  82.1 2.2 %place_q.1 = bf16[2,64,5120]{2,1,0:T(8,128)(2,1)} custom-call(s32[1]{0:T(128)} %bitcast.pos, s32[1]{0:T(128)S(6)} %copy.70.slot, bf16[64,2560]{1,0:T(8,128)(2,1)S(1)} %get-tuple-element.245.kept_own, bf16[64,2560]{1,0:T(8,128)(2,1)S(1)} %collective-permute-done.72.kept_other, bf16[64,7168]{1,0:T(8,128)(2,1)} %get-tuple-element.256.new.new_own), custom_call_target="tpu_custom_call" | custom-call | bytes 3145728 | tf_op jit(solution)/shard_map/place_q/pallas_call | solution.py:295
  84.3 0.0 collective-permute-done.73.other
  84.3 1.8 %place_kv.1 = (bf16[2,64,1024]{2,1,0:T(8,128)(2,1)}, bf16[2,64,1024]{2,1,0:T(8,128)(2,1)}) custom-call(s32[1]{0:T(128)} %bitcast.pos, s32[1]{0:T(128)S(6)} %copy.70.slot, bf16[64,1024]{1,0:T(8,128)(2,1)S(1)} %get-tuple-element.261.kept_own, bf16[64,7168]{1,0:T(8,128)(2,1)} %get-tuple-element.256.new.new_own, bf16[64,2048]{1,0:T(8,128)(2,1)S(1)} %collective-permute-done.73.other), custom_call_target="tpu_custom_call" | custom-call | bytes 2097152 | tf_op jit(solution)/shard_map/place_kv/pallas_call | solution.py:330
  (10 shorter events, 0.0 us)
Async XLA Ops:
  0.6 24.4 %copy-start = (bf16[2,64,5120]{2,1,0:T(8,128)(2,1)S(1)}, bf16[2,64,5120]{2,1,0:T(8,128)(2,1)}, u32[]{:S(2)}) copy-start(bf16[2,64,5120]{2,1,0:T(8,128)(2,1)} %qo.1) | copy-start | bytes 3932164
  1.4 1.0 %copy-start.3 = (bf16[2,64,1024]{2,1,0:T(8,128)(2,1)S(1)}, bf16[2,64,1024]{2,1,0:T(8,128)(2,1)}, u32[]{:S(2)}) copy-start(bf16[2,64,1024]{2,1,0:T(8,128)(2,1)} %k.3) | copy-start | bytes 786436
  2.3 0.9 %copy-start.4 = (bf16[2,64,1024]{2,1,0:T(8,128)(2,1)S(1)}, bf16[2,64,1024]{2,1,0:T(8,128)(2,1)}, u32[]{:S(2)}) copy-start(bf16[2,64,1024]{2,1,0:T(8,128)(2,1)} %v.3) | copy-start | bytes 786436
  3.3 0.7 copy-start.5
  4.1 2.8 %collective-permute-start.60 = (bf16[2,80,1024]{2,1,0:T(8,128)(2,1)S(1)}, bf16[2,80,1024]{2,1,0:T(8,128)(2,1)S(1)}, u32[]{:S(2)}, u32[]{:S(2)}) collective-permute-start(bf16[2,80,1024]{2,1,0:T(8,128)(2,1)S(1)} %pack_kv.1), channel_id=1, source_target_pairs={{0,1},{1,0},{2,3},{3,2},{4,5},{5,4},{6,7},{7,6},{8,9},{9,8},{10,11... | collective-permute-start | bytes 983048 | tf_op jit(solution)/shard_map/ppermute | solution.py:350
  6.9 11.0 %collective-permute-start.61 = (bf16[144,1024]{1,0:T(8,128)(2,1)S(1)}, bf16[144,1024]{1,0:T(8,128)(2,1)S(1)}, u32[]{:S(2)}, u32[]{:S(2)}) collective-permute-start(bf16[144,1024]{1,0:T(8,128)(2,1)S(1)} %get-tuple-element.228.k0.i0), channel_id=1, source_target_pairs={{0,2},{1,3},{2,4},{3,5},{4,6},{5,7},{6,0},{7,1},{8,10},{9,11},{10,... | collective-permute-start | bytes 884744 | tf_op jit(solution)/shard_map/ppermute | solution.py:355
  8.7 16.4 %collective-permute-start.62 = (bf16[144,1024]{1,0:T(8,128)(2,1)S(1)}, bf16[144,1024]{1,0:T(8,128)(2,1)S(1)}, u32[]{:S(2)}, u32[]{:S(2)}) collective-permute-start(bf16[144,1024]{1,0:T(8,128)(2,1)S(1)} %get-tuple-element.228.k0.i0), channel_id=1, source_target_pairs={{0,4},{1,5},{2,6},{3,7},{4,0},{5,1},{6,2},{7,3},{8,12},{9,13},{10,... | collective-permute-start | bytes 884744 | tf_op jit(solution)/shard_map/ppermute | solution.py:355
  12.0 13.1 %collective-permute-start.63 = (bf16[144,1024]{1,0:T(8,128)(2,1)S(1)}, bf16[144,1024]{1,0:T(8,128)(2,1)S(1)}, u32[]{:S(2)}, u32[]{:S(2)}) collective-permute-start(bf16[144,1024]{1,0:T(8,128)(2,1)S(1)} %get-tuple-element.228.k0.i0), channel_id=1, source_target_pairs={{0,6},{1,7},{2,0},{3,1},{4,2},{5,3},{6,4},{7,5},{8,14},{9,15},{10,... | collective-permute-start | bytes 884744 | tf_op jit(solution)/shard_map/ppermute | solution.py:355
  25.1 1.3 %copy-start.1 = (bf16[2,64,5120]{2,1,0:T(8,128)(2,1)S(1)}, bf16[2,64,5120]{2,1,0:T(8,128)(2,1)}, u32[]{:S(2)}) copy-start(bf16[2,64,5120]{2,1,0:T(8,128)(2,1)} %co.1) | copy-start | bytes 3932164
  26.4 5.6 %copy-start.2 = (bf16[2,64,5120]{2,1,0:T(8,128)(2,1)S(1)}, bf16[2,64,5120]{2,1,0:T(8,128)(2,1)}, u32[]{:S(2)}) copy-start(bf16[2,64,5120]{2,1,0:T(8,128)(2,1)} %co.1) | copy-start | bytes 3932164
  26.7 5.3 %collective-permute-start.64 = (bf16[2,2,64,2560]{3,2,1,0:T(8,128)(2,1)S(1)}, bf16[2,2,64,2560]{3,2,1,0:T(8,128)(2,1)S(1)}, u32[]{:S(2)}, u32[]{:S(2)}) collective-permute-start(bf16[2,2,64,2560]{3,2,1,0:T(8,128)(2,1)S(1)} %pack_q.1), channel_id=1, source_target_pairs={{0,1},{1,0},{2,3},{3,2},{4,5},{5,4},{6,7},{7,6},{8,9},{9,8},{10,11... | collective-permute-start | bytes 3932168 | tf_op jit(solution)/shard_map/ppermute | solution.py:350
  27.9 12.6 %collective-permute-start.68 = (bf16[128,1024]{1,0:T(8,128)(2,1)S(1)}, bf16[128,1024]{1,0:T(8,128)(2,1)S(1)}, u32[]{:S(2)}, u32[]{:S(2)}) collective-permute-start(bf16[128,1024]{1,0:T(8,128)(2,1)S(1)} %get-tuple-element.240.k0), channel_id=1, source_target_pairs={{0,2},{1,3},{2,4},{3,5},{4,6},{5,7},{6,0},{7,1},{8,10},{9,11},{10,... | collective-permute-start | bytes 786440 | tf_op jit(solution)/shard_map/ppermute | solution.py:355
  28.9 14.1 %collective-permute-start.69 = (bf16[128,1024]{1,0:T(8,128)(2,1)S(1)}, bf16[128,1024]{1,0:T(8,128)(2,1)S(1)}, u32[]{:S(2)}, u32[]{:S(2)}) collective-permute-start(bf16[128,1024]{1,0:T(8,128)(2,1)S(1)} %get-tuple-element.240.k0), channel_id=1, source_target_pairs={{0,4},{1,5},{2,6},{3,7},{4,0},{5,1},{6,2},{7,3},{8,12},{9,13},{10,... | collective-permute-start | bytes 786440 | tf_op jit(solution)/shard_map/ppermute | solution.py:355
  31.0 12.0 %collective-permute-start.70 = (bf16[128,1024]{1,0:T(8,128)(2,1)S(1)}, bf16[128,1024]{1,0:T(8,128)(2,1)S(1)}, u32[]{:S(2)}, u32[]{:S(2)}) collective-permute-start(bf16[128,1024]{1,0:T(8,128)(2,1)S(1)} %get-tuple-element.240.k0), channel_id=1, source_target_pairs={{0,6},{1,7},{2,0},{3,1},{4,2},{5,3},{6,4},{7,5},{8,14},{9,15},{10,... | collective-permute-start | bytes 786440 | tf_op jit(solution)/shard_map/ppermute | solution.py:355
  39.3 16.5 %collective-permute-start.71 = (bf16[64,2560]{1,0:T(8,128)(2,1)S(1)}, bf16[64,2560]{1,0:T(8,128)(2,1)S(1)}, u32[]{:S(2)}, u32[]{:S(2)}) collective-permute-start(bf16[64,2560]{1,0:T(8,128)(2,1)S(1)} %get-tuple-element.239), channel_id=1, source_target_pairs={{0,1},{1,0},{2,3},{3,2},{4,5},{5,4},{6,7},{7,6},{8,9},{9,8},{10,11... | collective-permute-start | bytes 983048 | tf_op jit(solution)/shard_map/ppermute | solution.py:350
  40.3 12.5 %collective-permute-start.65 = (bf16[128,1024]{1,0:T(8,128)(2,1)S(1)}, bf16[128,1024]{1,0:T(8,128)(2,1)S(1)}, u32[]{:S(2)}, u32[]{:S(2)}) collective-permute-start(bf16[128,1024]{1,0:T(8,128)(2,1)S(1)} %get-tuple-element.233), channel_id=1, source_target_pairs={{0,6},{1,7},{2,0},{3,1},{4,2},{5,3},{6,4},{7,5},{8,14},{9,15},{10,... | collective-permute-start | bytes 786440 | tf_op jit(solution)/shard_map/ppermute | solution.py:355
  40.5 12.3 %collective-permute-start.66 = (bf16[128,1024]{1,0:T(8,128)(2,1)S(1)}, bf16[128,1024]{1,0:T(8,128)(2,1)S(1)}, u32[]{:S(2)}, u32[]{:S(2)}) collective-permute-start(bf16[128,1024]{1,0:T(8,128)(2,1)S(1)} %get-tuple-element.234), channel_id=1, source_target_pairs={{0,4},{1,5},{2,6},{3,7},{4,0},{5,1},{6,2},{7,3},{8,12},{9,13},{10,... | collective-permute-start | bytes 786440 | tf_op jit(solution)/shard_map/ppermute | solution.py:355
  43.0 12.8 %collective-permute-start.67 = (bf16[128,1024]{1,0:T(8,128)(2,1)S(1)}, bf16[128,1024]{1,0:T(8,128)(2,1)S(1)}, u32[]{:S(2)}, u32[]{:S(2)}) collective-permute-start(bf16[128,1024]{1,0:T(8,128)(2,1)S(1)} %get-tuple-element.235), channel_id=1, source_target_pairs={{0,2},{1,3},{2,4},{3,5},{4,6},{5,7},{6,0},{7,1},{8,10},{9,11},{10,... | collective-permute-start | bytes 786440 | tf_op jit(solution)/shard_map/ppermute | solution.py:355
  50.4 31.7 %collective-permute-start.72 = (bf16[64,2560]{1,0:T(8,128)(2,1)S(1)}, bf16[64,2560]{1,0:T(8,128)(2,1)S(1)}, u32[]{:S(2)}, u32[]{:S(2)}) collective-permute-start(bf16[64,2560]{1,0:T(8,128)(2,1)S(1)} %get-tuple-element.246), channel_id=1, source_target_pairs={{0,1},{1,0},{2,3},{3,2},{4,5},{5,4},{6,7},{7,6},{8,9},{9,8},{10,11... | collective-permute-start | bytes 983048 | tf_op jit(solution)/shard_map/ppermute | solution.py:350
  56.3 23.1 %collective-permute-start.28 = (bf16[64,7168]{1,0:T(8,128)(2,1)S(1)}, bf16[64,7168]{1,0:T(8,128)(2,1)}, u32[]{:S(2)}, u32[]{:S(2)}) collective-permute-start(bf16[64,7168]{1,0:T(8,128)(2,1)S(1)} %get-tuple-element.148), channel_id=1, source_target_pairs={{0,64},{8,72},{16,80},{24,88},{32,96},{40,104},{48,112},{56,120},{... | collective-permute-start | bytes 2752520 | tf_op jit(solution)/shard_map/cond/branch_7_fun/ppermute | solution.py:363
  59.1 7.2 %collective-permute-start.29 = (bf16[128,1024]{1,0:T(8,128)(2,1)S(1)}, bf16[128,1024]{1,0:T(8,128)(2,1)}, u32[]{:S(2)}, u32[]{:S(2)}) collective-permute-start(bf16[128,1024]{1,0:T(8,128)(2,1)S(1)} %get-tuple-element.149), channel_id=1, source_target_pairs={{0,6},{1,7},{2,0},{3,1},{4,2},{5,3},{6,4},{7,5},{8,14},{9,15},{10,... | collective-permute-start | bytes 786440 | tf_op jit(solution)/shard_map/cond/branch_7_fun/ppermute | solution.py:355
  60.0 7.9 %collective-permute-start.30 = (bf16[128,1024]{1,0:T(8,128)(2,1)S(1)}, bf16[128,1024]{1,0:T(8,128)(2,1)}, u32[]{:S(2)}, u32[]{:S(2)}) collective-permute-start(bf16[128,1024]{1,0:T(8,128)(2,1)S(1)} %get-tuple-element.150), channel_id=1, source_target_pairs={{0,4},{1,5},{2,6},{3,7},{4,0},{5,1},{6,2},{7,3},{8,12},{9,13},{10,... | collective-permute-start | bytes 786440 | tf_op jit(solution)/shard_map/cond/branch_7_fun/ppermute | solution.py:355
  60.9 14.6 %collective-permute-start.31 = (bf16[128,1024]{1,0:T(8,128)(2,1)S(1)}, bf16[128,1024]{1,0:T(8,128)(2,1)}, u32[]{:S(2)}, u32[]{:S(2)}) collective-permute-start(bf16[128,1024]{1,0:T(8,128)(2,1)S(1)} %get-tuple-element.151), channel_id=1, source_target_pairs={{0,2},{1,3},{2,4},{3,5},{4,6},{5,7},{6,0},{7,1},{8,10},{9,11},{10,... | collective-permute-start | bytes 786440 | tf_op jit(solution)/shard_map/cond/branch_7_fun/ppermute | solution.py:355
  80.7 3.7 %collective-permute-start.73 = (bf16[64,2048]{1,0:T(8,128)(2,1)S(1)}, bf16[64,2048]{1,0:T(8,128)(2,1)S(1)}, u32[]{:S(2)}, u32[]{:S(2)}) collective-permute-start(bf16[64,2048]{1,0:T(8,128)(2,1)S(1)} %get-tuple-element.262), channel_id=1, source_target_pairs={{0,1},{1,0},{2,3},{3,2},{4,5},{5,4},{6,7},{7,6},{8,9},{9,8},{10,11... | collective-permute-start | bytes 786440 | tf_op jit(solution)/shard_map/ppermute | solution.py:350

commit v2 on v1

--- a/solution.py
+++ b/solution.py
@@ -26,6 +26,7 @@
 BF = jnp.bfloat16
 F32 = jnp.float32
 VMEM_LIMIT = 16 * 1024 * 1024
+ORDER = (0, 1, 3, 2)
 SMALL_LIMIT = 8 * 1024 * 1024
 
 
@@ -97,15 +98,16 @@
     )(*where, queries, cotangent)
 
 
-def chunks_kernel(pos, slot, k, v, ids, got, out_h, out_k):
+def chunks_kernel(pos, slot, k, v, ids, got, top, bottom, out_k):
     first = lax.broadcasted_iota(jnp.int32, (16, DH), 1) < TOK
-    for i, out in enumerate((out_h, out_k)):
+    for i, out in enumerate((top, out_k)):
         span = span_of(slot, i)
         interleave(out, slice(0, TOK), k.at[span], v.at[span])
-        out[TOK:CHUNK, :] = got[i, :TOK, :]
         theirs = got[i, TOK : TOK + 16, 0:DH].astype(F32)
         both = jnp.where(first, id_tile(ids, slot, i), theirs).astype(BF)
-        out_h[CHUNK : CHUNK + 16, i * DH : (i + 1) * DH] = both
+        bottom[TOK : TOK + 16, i * DH : (i + 1) * DH] = both
+    bottom[0:TOK, :] = got[0, :TOK, :]
+    out_k[TOK:CHUNK, :] = got[1, :TOK, :]
 
 
 def make_chunks(where, key_rows, value_rows, episodes, got):
@@ -122,12 +124,14 @@
                 pl.BlockSpec((2, TOK + 16, KVW), lambda i, p, s: (0, 0, 0)),
             ],
             out_specs=[
-                pl.BlockSpec((CHUNK + 16, KVW), lambda i, p, s: (0, 0)),
+                pl.BlockSpec((TOK, KVW), lambda i, p, s: (0, 0)),
+                pl.BlockSpec((TOK + 16, KVW), lambda i, p, s: (0, 0)),
                 pl.BlockSpec((CHUNK, KVW), lambda i, p, s: (0, 0)),
             ],
         ),
         out_shape=[
-            jax.ShapeDtypeStruct((CHUNK + 16, KVW), BF),
+            jax.ShapeDtypeStruct((TOK, KVW), BF),
+            jax.ShapeDtypeStruct((TOK + 16, KVW), BF),
             jax.ShapeDtypeStruct((CHUNK, KVW), BF),
         ],
         cost_estimate=pl.CostEstimate(flops=0, bytes_accessed=2 << 20, transcendentals=0),
@@ -136,10 +140,9 @@
     )(*where, key_rows, value_rows, episodes, got)
 
 
-def attention_kernel(
-    pos, slot, qo, co, qx, k0, k1, k2, k3, i0, i1, i2, i3,
-    gqo, gqx, p0, p1, p2, p3, bias, st, dt, pt, ds,
-):
+def attention_kernel(pos, slot, qo, co, qx, *refs):
+    pieces = refs[:-15]
+    i0, i1, i2, i3, gqo, gqx, p0, p1, p2, p3, bias, st, dt, pt, ds = refs[-15:]
     chip = pos[0] >> 1
     core = core_of(pos)
 
@@ -149,13 +152,14 @@
         lanes = lax.broadcasted_iota(jnp.int32, (CHUNK, CHUNK), 1)
         query_pos = chip * CHUNK + ((lanes + core * TOK) & (CHUNK - 1))
         query_id = jnp.broadcast_to(i0[0:1, :].astype(F32), (CHUNK, CHUNK))
-        for d, ids in enumerate((i0, i1, i2, i3)):
+        for at, ids in enumerate((i0, i1, i2, i3)):
+            d = ORDER[at]
             key_pos = ((chip - d) & (CHIPS - 1)) * CHUNK + ((rows + core * TOK) & (CHUNK - 1))
             key_id = jnp.broadcast_to(ids[0:1, :].astype(F32), (CHUNK, CHUNK)).T
             allowed = (key_id == query_id) & (key_pos <= query_pos)
-            bias[d * CHUNK : (d + 1) * CHUNK, :] = jnp.where(allowed, 0.0, -1e30).astype(F32)
-
-    kv = [k[0:CHUNK, :] for k in (k0, k1, k2, k3)]
+            bias[at * CHUNK : (at + 1) * CHUNK, :] = jnp.where(allowed, 0.0, -1e30).astype(F32)
+
+    kv = [piece[...] for piece in pieces]
     keys = jnp.concatenate([x[:, :DH] for x in kv], axis=0)
     values = jnp.concatenate([x[:, DH:] for x in kv], axis=0)
 
@@ -198,14 +202,15 @@
     own = pl.BlockSpec((1, TOK, GROUPS * DH), lambda g, p, s: (span_of(s, which), 0, core_of(p) * LOCAL_KV + g))
     other = pl.BlockSpec((1, 2, TOK, GROUPS * DH), lambda g, p, s: (which, 0, 0, g))
     chunk = pl.BlockSpec((CHUNK, 2 * DH), lambda g, p, s: (0, g))
-    ids = pl.BlockSpec((16, DH), lambda g, p, s: (CHUNK // 16, which))
+    piece = pl.BlockSpec((KEYS // len(chunks), 2 * DH), lambda g, p, s: (0, g))
+    ids = pl.BlockSpec((16, DH), lambda g, p, s: (TOK // 16, which))
     out_q = pl.BlockSpec((TOK, GROUPS * DH), lambda g, p, s: (0, g))
     return pl.pallas_call(
         attention_kernel,
         grid_spec=pltpu.PrefetchScalarGridSpec(
             num_scalar_prefetch=2,
             grid=(LOCAL_KV,),
-            in_specs=[own, own, other] + [chunk] * 4 + [ids] * 4,
+            in_specs=[own, own, other] + [piece] * len(chunks) + [ids] * 4,
             out_specs=[out_q, out_q] + [chunk] * 4,
             scratch_shapes=[
                 pltpu.VMEM((KEYS, CHUNK), F32),
@@ -253,29 +258,20 @@
     )(*parts, gq_own, gq_got)
 
 
-def keep_kernel(p0, r1, r2, r3, new, own, swap):
+def keep_kernel(p0, r1, r2, r3, own, other):
     total = total_of(p0, r1, r2, r3)
     own[...] = total[:TOK]
-    swap[:, :KVW] = total[TOK:]
-    swap[:, KVW:] = new[...]
-
-
-def keep(parts, new):
-    whole = lambda shape: pl.BlockSpec(shape, lambda i: (0, 0))
+    other[...] = total[TOK:]
+
+
+def keep(parts):
     return pl.pallas_call(
         keep_kernel,
-        grid=(1,),
-        in_specs=[whole((CHUNK, KVW))] * 4
-        + [pl.BlockSpec((TOK, KVW), lambda i: (0, 2 * QW // KVW + 1))],
-        out_specs=[whole((TOK, KVW)), whole((TOK, 2 * KVW))],
-        out_shape=[
-            jax.ShapeDtypeStruct((TOK, KVW), BF),
-            jax.ShapeDtypeStruct((TOK, 2 * KVW), BF),
-        ],
+        out_shape=[jax.ShapeDtypeStruct((TOK, KVW), BF)] * 2,
         compiler_params=pltpu.CompilerParams(vmem_limit_bytes=SMALL_LIMIT),
         cost_estimate=pl.CostEstimate(flops=0, bytes_accessed=2 << 20, transcendentals=0),
         name="keep",
-    )(*parts, new)
+    )(*parts)
 
 
 def place_q_kernel(pos, slot, kept_own, kept_other, new, out):
@@ -308,25 +304,25 @@
     )(*where, kept_own, kept_other, new)
 
 
-def place_kv_kernel(pos, slot, kept_own, new_own, other, out_k, out_v):
+def place_kv_kernel(pos, slot, kept_own, new_own, kept_other, new_other, out_k, out_v):
     for core in range(2):
 
         @pl.when(core_of(pos) == core)
         def _():
-            for slot_out, at, part, start in (
-                (0, core, kept_own, 0),
-                (0, 1 - core, other, 0),
-                (1, core, new_own, 0),
-                (1, 1 - core, other, KVW),
+            for slot_out, at, part in (
+                (0, core, kept_own),
+                (0, 1 - core, kept_other),
+                (1, core, new_own),
+                (1, 1 - core, new_other),
             ):
                 for g in range(LOCAL_KV):
                     to = slice(at * KW + g * DH, at * KW + (g + 1) * DH)
-                    mid = start + (2 * g + 1) * DH
+                    mid = (2 * g + 1) * DH
                     out_k[slot_out, :, to] = part[:, mid - DH : mid]
                     out_v[slot_out, :, to] = part[:, mid : mid + DH]
 
 
-def place_kv(where, kept_own, new, other):
+def place_kv(where, kept_own, new, kept_other, new_other):
     return pl.pallas_call(
         place_kv_kernel,
         grid_spec=pltpu.PrefetchScalarGridSpec(
@@ -335,7 +331,8 @@
             in_specs=[
                 pl.BlockSpec((TOK, KVW), lambda i, p, s: (0, 0)),
                 pl.BlockSpec((TOK, KVW), lambda i, p, s: (0, 2 * QW // KVW)),
-                pl.BlockSpec((TOK, 2 * KVW), lambda i, p, s: (0, 0)),
+                pl.BlockSpec((TOK, KVW), lambda i, p, s: (0, 0)),
+                pl.BlockSpec((TOK, KVW), lambda i, p, s: (0, 0)),
             ],
             out_specs=[pl.BlockSpec((2, TOK, 2 * KW), lambda i, p, s: (0, 0, 0))] * 2,
         ),
@@ -343,7 +340,7 @@
         cost_estimate=pl.CostEstimate(flops=0, bytes_accessed=2 << 20, transcendentals=0),
         compiler_params=pltpu.CompilerParams(vmem_limit_bytes=SMALL_LIMIT),
         name="place_kv",
-    )(*where, kept_own, new, other)
+    )(*where, kept_own, new, kept_other, new_other)
 
 
 def core_swap(x):
@@ -355,42 +352,45 @@
     return lax.ppermute(x, "seq", [(i, (i + 2 * d) % n) for i in range(n)])
 
 
-def trade(swap_mask, handed, sends):
+def trade(swap_mask, handed, parts):
     replicas = lax.axis_size("dp")
 
-    def branch(mask, handed, sends):
-        sums = [ring(x, -d - 1) for d, x in enumerate(sends)]
-        return lax.ppermute(handed, "dp", [(r, r ^ mask) for r in range(replicas)]), sums
+    def branch(mask, handed, parts):
+        sums = [ring(x, -d) for x, d in zip(parts[1:], ORDER[1:])]
+        new = lax.ppermute(handed, "dp", [(r, r ^ mask) for r in range(replicas)])
+        return new, keep([parts[0]] + sums)
 
     branches = [functools.partial(branch, mask) for mask in range(1, replicas)]
-    return lax.switch(swap_mask[0] - 1, branches, handed, sends)
+    return lax.switch(swap_mask[0] - 1, branches, handed, parts)
 
 
 def per_device(queries, key_rows, value_rows, cotangent, episodes, send_slot, swap_mask):
     tied = lax.optimization_barrier
     where = (lax.axis_index("seq").reshape(1).astype(jnp.int32), send_slot)
     got = core_swap(pack_kv(where, key_rows, value_rows, episodes))
-    chunk_h, chunk_k = make_chunks(where, key_rows, value_rows, episodes, got)
-    chunks_h = [chunk_h] + [ring(chunk_h, d) for d in range(1, CHIPS)]
-    *chunks_h, chunk_k, queries, cotangent = tied((*chunks_h, chunk_k, queries, cotangent))
+    top, bottom, chunk_k = make_chunks(where, key_rows, value_rows, episodes, got)
+    top_1, bottom_3, bottom_1, top_3 = ring(top, 1), ring(bottom, 3), ring(bottom, 1), ring(top, 3)
+    top_2, bottom_2 = ring(top_1, 1), ring(bottom_3, 3)
+    pieces = (top, bottom, top_1, bottom_1, top_3, bottom_3, top_2, bottom_2)
+    *pieces, chunk_k, queries, cotangent = tied((*pieces, chunk_k, queries, cotangent))
     q_other = core_swap(pack_q(where, queries, cotangent))
-    chunks_k = [chunk_k] + [ring(chunk_k, d) for d in range(1, CHIPS)]
+    chunks_k = [chunk_k] + [ring(chunk_k, d) for d in ORDER[1:]]
 
     gq_own, gq_other, *parts = attention(
-        where, 0, queries, cotangent, q_other, chunks_h, chunks_h
+        where, 0, queries, cotangent, q_other, pieces, pieces[1::2]
     )
-    sums = [parts[0]] + [ring(parts[d], -d) for d in range(1, CHIPS)]
+    sums = [parts[0]] + [ring(x, -d) for x, d in zip(parts[1:], ORDER[1:])]
     gq_got = core_swap(gq_other)
     *chunks_k, gq_own = tied((*chunks_k, gq_own))
     kept_own, kept_other, *parts = attention(
-        where, 1, queries, cotangent, q_other, chunks_k, chunks_h
+        where, 1, queries, cotangent, q_other, chunks_k, pieces[1::2]
     )
     *sums, gq_own, gq_got, kept_own = tied((*sums, gq_own, gq_got, kept_own))
-    new, sums = trade(swap_mask, hand_over(sums, gq_own, gq_got), parts[1:])
-    kv_own, kv_other = keep([parts[0]] + sums, new)
+    new, (kv_own, kv_other) = trade(swap_mask, hand_over(sums, gq_own, gq_got), parts)
     kept_other, kv_other = core_swap(kept_other), core_swap(kv_other)
+    kv_new = core_swap(new[:, 2 * QW + KVW :])
     grad_queries = place_q(where, kept_own, kept_other, new)
-    grad_keys, grad_values = place_kv(where, kv_own, new, kv_other)
+    grad_keys, grad_values = place_kv(where, kv_own, new, kv_other, kv_new)
     return grad_queries, grad_keys, grad_values
 
 

time: 86.9 us -> 83.5 us (0.961)
  waiting for transfers between devices: 34.9 us -> 26.3 us
  starting transfers between devices: 24.4 us -> 29 us
  Pallas kernels: 20.5 us -> 19.5 us
  local copies, waits for them, and re-layouts: 3.89 us -> 4.8 us
    ppermute x12 -> x15, waiting for transfers between devices: 29.6 us -> 20.1 us  [ring(): return lax.ppermute(x, 'seq', [(i, (i + 2 * d) % n) for i in range(n)])]
    ppermute x12 -> x15, starting transfers between devices: 14.6 us -> 19.3 us  [ring(): return lax.ppermute(x, 'seq', [(i, (i + 2 * d) % n) for i in range(n)])]
    ppermute x1, starting transfers between devices: 2.82 us -> 1.28 us  [branch(): new = lax.ppermute(handed, 'dp', [(r, r ^ mask) for r in range(replicas)])]
    ppermute x5 -> x6, starting transfers between devices: 6.96 us -> 8.48 us  [core_swap(): return lax.ppermute(x, 'seq', [(i, i ^ 1) for i in range(2 * CHIPS)])]
    pallas_call x1, Pallas kernels: 1.26 us -> 0.11 us  [keep(): pl.pallas_call(keep_kernel, out_shape=[jax.ShapeDtypeStruct((TOK, KVW), B...]
    ppermute x1, waiting for transfers between devices: 3.97 us -> 4.9 us  [branch(): new = lax.ppermute(handed, 'dp', [(r, r ^ mask) for r in range(replicas)])]
    slice x0 -> x1, local copies, waits for them, and re-layouts: none -> 0.91 us  [per_device(): kv_new = core_swap(new[:, 2 * QW + KVW:])]
  transfers between devices with their start and end apart: 18 -> 22, of which waited for: 9 -> 9; matrix products, arithmetic and copies ran while one was open for 0% -> 1% of each run, Pallas kernels for 21% -> 21%
where the time goes in v2:
time: 83.5 us; the launch traced here: 82 us
  starting transfers between devices  29 us (35%)
  waiting for transfers between devices  26.3 us (31%)
  Pallas kernels  19.5 us (23%)
  local copies, waits for them, and re-layouts  4.8 us (6%)
  between operations  2.17 us (3%)
    ppermute x15, waiting for transfers between devices, ring(): return lax.ppermute(x, 'seq', [(i, (i + 2 * d) % n) for i in range(n)])  20.1 us
    ppermute x15, starting transfers between devices, ring(): return lax.ppermute(x, 'seq', [(i, (i + 2 * d) % n) for i in range(n)])  19.3 us
    pallas_call x2, Pallas kernels, attention(): pl.pallas_call(attention_kernel, grid_spec=pltpu.PrefetchScalarGridSpec(n...  14.8 us
    ppermute x6, starting transfers between devices, core_swap(): return lax.ppermute(x, 'seq', [(i, i ^ 1) for i in range(2 * CHIPS)])  8.48 us
    ppermute x1, waiting for transfers between devices, branch(): new = lax.ppermute(handed, 'dp', [(r, r ^ mask) for r in range(replicas)])  4.9 us
    unnamed x12, local copies, waits for them, and re-layouts  3.89 us
    pallas_call x1, Pallas kernels, place_q(): pl.pallas_call(place_q_kernel, grid_spec=pltpu.PrefetchScalarGridSpec(num...  2.23 us
    pallas_call x1, Pallas kernels, place_kv(): pl.pallas_call(place_kv_kernel, grid_spec=pltpu.PrefetchScalarGridSpec(nu...  1.81 us
  transfers between devices with their start and end apart: 22, of which 9 were waited for; matrix products, arithmetic and copies ran while one was open for 1% of the time, Pallas kernels for 21%

profile of v2, /device:TPU:1, one launch (start us, length us, event | category | flops | bytes accessed | tf_op | source)
XLA Modules:
  0.0 82.0 jit_solution(16180632465262634337)
XLA Ops:
  1.4 0.9 %copy-done.3 = bf16[2,64,1024]{2,1,0:T(8,128)(2,1)S(1)} copy-done((bf16[2,64,1024]{2,1,0:T(8,128)(2,1)S(1)}, bf16[2,64,1024]{2,1,0:T(8,128)(2,1)}, u32[]{:S(2)}) %copy-start.3) | copy-done | bytes 262168
  2.3 0.9 %copy-done.4 = bf16[2,64,1024]{2,1,0:T(8,128)(2,1)S(1)} copy-done((bf16[2,64,1024]{2,1,0:T(8,128)(2,1)S(1)}, bf16[2,64,1024]{2,1,0:T(8,128)(2,1)}, u32[]{:S(2)}) %copy-start.4) | copy-done | bytes 262168
  3.3 0.7 copy-done.5
  4.0 0.1 pack_kv.1
  4.1 1.5 %collective-permute-start.60 = (bf16[2,80,1024]{2,1,0:T(8,128)(2,1)S(1)}, bf16[2,80,1024]{2,1,0:T(8,128)(2,1)S(1)}, u32[]{:S(2)}, u32[]{:S(2)}) collective-permute-start(bf16[2,80,1024]{2,1,0:T(8,128)(2,1)S(1)} %pack_kv.1), channel_id=1, source_target_pairs={{0,1},{1,0},{2,3},{3,2},{4,5},{5,4},{6,7},{7,6},{8,9},{9,8},{10,11... | collective-permute-start | bytes 983048 | tf_op jit(solution)/shard_map/ppermute | solution.py:347
  5.6 1.3 %collective-permute-done.60.got = bf16[2,80,1024]{2,1,0:T(8,128)(2,1)S(1)} collective-permute-done((bf16[2,80,1024]{2,1,0:T(8,128)(2,1)S(1)}, bf16[2,80,1024]{2,1,0:T(8,128)(2,1)S(1)}, u32[]{:S(2)}, u32[]{:S(2)}) %collective-permute-start.60) | collective-permute-done | bytes 327712 | tf_op jit(solution)/shard_map/ppermute | solution.py:347
  6.8 0.1 make_chunks.1
  6.9 3.9 %collective-permute-start.64 = (bf16[80,1024]{1,0:T(8,128)(2,1)S(1)}, bf16[80,1024]{1,0:T(8,128)(2,1)S(1)}, u32[]{:S(2)}, u32[]{:S(2)}) collective-permute-start(bf16[80,1024]{1,0:T(8,128)(2,1)S(1)} %get-tuple-element.307.refs_1_.refs_8_.refs_4_), channel_id=1, source_target_pairs={{0,6},{1,7},{2,0},{3,1},{4,2},{5,3},{6,4},{7,5},{8,14},{9,15},{10,... | collective-permute-start | bytes 491528 | tf_op jit(solution)/shard_map/ppermute | solution.py:352
  10.8 3.2 %collective-permute-done.64.refs_5_.refs_10_.refs_6_ = bf16[80,1024]{1,0:T(8,128)(2,1)S(1)} collective-permute-done((bf16[80,1024]{1,0:T(8,128)(2,1)S(1)}, bf16[80,1024]{1,0:T(8,128)(2,1)S(1)}, u32[]{:S(2)}, u32[]{:S(2)}) %collective-permute-start.64) | collective-permute-done | bytes 163872 | tf_op jit(solution)/shard_map/ppermute | solution.py:352
  14.0 3.4 %collective-permute-start.66 = (bf16[80,1024]{1,0:T(8,128)(2,1)S(1)}, bf16[80,1024]{1,0:T(8,128)(2,1)S(1)}, u32[]{:S(2)}, u32[]{:S(2)}) collective-permute-start(bf16[80,1024]{1,0:T(8,128)(2,1)S(1)} %collective-permute-done.64.refs_5_.refs_10_.refs_6_), channel_id=1, source_target_pairs={{0,6},{1,7},{2,0},{3,1},{4,2},{5,3},{6,4},{7,5},{8,14},{9,15},{10,... | collective-permute-start | bytes 491528 | tf_op jit(solution)/shard_map/ppermute | solution.py:352
  17.4 0.0 collective-permute-start.63
  17.5 0.0 collective-permute-done.61.refs_2_
  17.5 1.4 %collective-permute-start.65 = (bf16[64,1024]{1,0:T(8,128)(2,1)S(1)}, bf16[64,1024]{1,0:T(8,128)(2,1)S(1)}, u32[]{:S(2)}, u32[]{:S(2)}) collective-permute-start(bf16[64,1024]{1,0:T(8,128)(2,1)S(1)} %collective-permute-done.61.refs_2_), channel_id=1, source_target_pairs={{0,2},{1,3},{2,4},{3,5},{4,6},{5,7},{6,0},{7,1},{8,10},{9,11},{10,... | collective-permute-start | bytes 393224 | tf_op jit(solution)/shard_map/ppermute | solution.py:352
  18.9 3.6 %collective-permute-done.63.refs_4_ = bf16[64,1024]{1,0:T(8,128)(2,1)S(1)} collective-permute-done((bf16[64,1024]{1,0:T(8,128)(2,1)S(1)}, bf16[64,1024]{1,0:T(8,128)(2,1)S(1)}, u32[]{:S(2)}, u32[]{:S(2)}) %collective-permute-start.63) | collective-permute-done | bytes 131104 | tf_op jit(solution)/shard_map/ppermute | solution.py:352
  22.5 0.0 collective-permute-done.65.refs_6_
  22.5 0.0 collective-permute-done.66.refs_7_.refs_11_
  22.6 0.0 copy-start.1
  22.6 1.3 %copy-done.1 = bf16[2,64,5120]{2,1,0:T(8,128)(2,1)S(1)} copy-done((bf16[2,64,5120]{2,1,0:T(8,128)(2,1)S(1)}, bf16[2,64,5120]{2,1,0:T(8,128)(2,1)}, u32[]{:S(2)}) %copy-start.1) | copy-done | bytes 1310744
  23.9 0.3 pack_q.1
  24.2 2.8 %collective-permute-start.67 = (bf16[2,2,64,2560]{3,2,1,0:T(8,128)(2,1)S(1)}, bf16[2,2,64,2560]{3,2,1,0:T(8,128)(2,1)S(1)}, u32[]{:S(2)}, u32[]{:S(2)}) collective-permute-start(bf16[2,2,64,2560]{3,2,1,0:T(8,128)(2,1)S(1)} %pack_q.1), channel_id=1, source_target_pairs={{0,1},{1,0},{2,3},{3,2},{4,5},{5,4},{6,7},{7,6},{8,9},{9,8},{10,11... | collective-permute-start | bytes 3932168 | tf_op jit(solution)/shard_map/ppermute | solution.py:347
  26.9 0.4 collective-permute-start.71
  27.3 2.4 %collective-permute-start.72 = (bf16[128,1024]{1,0:T(8,128)(2,1)S(1)}, bf16[128,1024]{1,0:T(8,128)(2,1)S(1)}, u32[]{:S(2)}, u32[]{:S(2)}) collective-permute-start(bf16[128,1024]{1,0:T(8,128)(2,1)S(1)} %get-tuple-element.322.refs_0_), channel_id=1, source_target_pairs={{0,6},{1,7},{2,0},{3,1},{4,2},{5,3},{6,4},{7,5},{8,14},{9,15},{10,... | collective-permute-start | bytes 786440 | tf_op jit(solution)/shard_map/ppermute | solution.py:352
  29.8 1.2 %collective-permute-start.73 = (bf16[128,1024]{1,0:T(8,128)(2,1)S(1)}, bf16[128,1024]{1,0:T(8,128)(2,1)S(1)}, u32[]{:S(2)}, u32[]{:S(2)}) collective-permute-start(bf16[128,1024]{1,0:T(8,128)(2,1)S(1)} %get-tuple-element.322.refs_0_), channel_id=1, source_target_pairs={{0,4},{1,5},{2,6},{3,7},{4,0},{5,1},{6,2},{7,3},{8,12},{9,13},{10,... | collective-permute-start | bytes 786440 | tf_op jit(solution)/shard_map/ppermute | solution.py:352
  31.0 0.0 collective-permute-done.67.qx
  31.0 7.4 %attention.2 = (bf16[64,2560]{1,0:T(8,128)(2,1)S(1)}, bf16[64,2560]{1,0:T(8,128)(2,1)S(1)}, f32[128,1024]{1,0:T(8,128)S(1)}, bf16[128,1024]{1,0:T(8,128)(2,1)S(1...) custom-call(s32[1]{0:T(128)} %bitcast.pos, s32[1]{0:T(128)S(6)} %copy.55.slot, ...), custom_call_target="tpu_custom_call" | custom-call | flops 1677721600 | bytes 5242880 | tf_op jit(solution)/shard_map/attention/pallas_call | solution.py:208
  38.4 1.5 %collective-permute-start.68 = (bf16[128,1024]{1,0:T(8,128)(2,1)S(1)}, bf16[128,1024]{1,0:T(8,128)(2,1)S(1)}, u32[]{:S(2)}, u32[]{:S(2)}) collective-permute-start(bf16[128,1024]{1,0:T(8,128)(2,1)S(1)} %get-tuple-element.315), channel_id=1, source_target_pairs={{0,6},{1,7},{2,0},{3,1},{4,2},{5,3},{6,4},{7,5},{8,14},{9,15},{10,... | collective-permute-start | bytes 786440 | tf_op jit(solution)/shard_map/ppermute | solution.py:352
  39.9 0.0 collective-permute-start.69
  40.0 1.8 %collective-permute-start.70 = (bf16[128,1024]{1,0:T(8,128)(2,1)S(1)}, bf16[128,1024]{1,0:T(8,128)(2,1)S(1)}, u32[]{:S(2)}, u32[]{:S(2)}) collective-permute-start(bf16[128,1024]{1,0:T(8,128)(2,1)S(1)} %get-tuple-element.317), channel_id=1, source_target_pairs={{0,4},{1,5},{2,6},{3,7},{4,0},{5,1},{6,2},{7,3},{8,12},{9,13},{10,... | collective-permute-start | bytes 786440 | tf_op jit(solution)/shard_map/ppermute | solution.py:352
  41.7 1.2 %collective-permute-done.73.refs_3_ = bf16[128,1024]{1,0:T(8,128)(2,1)S(1)} collective-permute-done((bf16[128,1024]{1,0:T(8,128)(2,1)S(1)}, bf16[128,1024]{1,0:T(8,128)(2,1)S(1)}, u32[]{:S(2)}, u32[]{:S(2)}) %collective-permute-start.73) | collective-permute-done | bytes 262176 | tf_op jit(solution)/shard_map/ppermute | solution.py:352
  43.0 1.3 %collective-permute-start.74 = (bf16[64,2560]{1,0:T(8,128)(2,1)S(1)}, bf16[64,2560]{1,0:T(8,128)(2,1)S(1)}, u32[]{:S(2)}, u32[]{:S(2)}) collective-permute-start(bf16[64,2560]{1,0:T(8,128)(2,1)S(1)} %get-tuple-element.321), channel_id=1, source_target_pairs={{0,1},{1,0},{2,3},{3,2},{4,5},{5,4},{6,7},{7,6},{8,9},{9,8},{10,11... | collective-permute-start | bytes 983048 | tf_op jit(solution)/shard_map/ppermute | solution.py:347
  44.2 7.3 %attention.3 = (bf16[64,2560]{1,0:T(8,128)(2,1)S(1)}, bf16[64,2560]{1,0:T(8,128)(2,1)S(1)}, f32[128,1024]{1,0:T(8,128)S(1)}, bf16[128,1024]{1,0:T(8,128)(2,1)S(1...) custom-call(s32[1]{0:T(128)} %bitcast.pos, s32[1]{0:T(128)S(6)} %copy.55.slot, ...), custom_call_target="tpu_custom_call" | custom-call | flops 1677721600 | bytes 5242880 | tf_op jit(solution)/shard_map/attention/pallas_call | solution.py:208
  51.6 0.1 collective-permute-start.75
  52.3 1.3 %collective-permute-done.70.r3 = bf16[128,1024]{1,0:T(8,128)(2,1)S(1)} collective-permute-done((bf16[128,1024]{1,0:T(8,128)(2,1)S(1)}, bf16[128,1024]{1,0:T(8,128)(2,1)S(1)}, u32[]{:S(2)}, u32[]{:S(2)}) %collective-permute-start.70) | collective-permute-done | bytes 262176 | tf_op jit(solution)/shard_map/ppermute | solution.py:352
  53.6 0.2 hand_over.1
  53.8 20.4 %conditional.1 = (bf16[64,7168]{1,0:T(8,128)(2,1)}, bf16[64,1024]{1,0:T(8,128)(2,1)S(1)}, bf16[64,1024]{1,0:T(8,128)(2,1)S(1)}) conditional(s32[]{:T(128)} %bitcast.1, (bf16[64,7168]{1,0:T(8,128)(2,1)S(1)}, bf16[128,1024]{1,0:T(8,128)(2,1)S(1)}, bf16[128,1024]{1,0:T(8,128)(2,1)S(1)}, bf16[128,1024]{1,0:T(8,128)(2,1)S(1)}, ...), branch_computations={%region_0.0_spmd, %region_1.0_spmd, %region_2.0_spmd, %region_3.0_... | conditional | bytes 8913080 | solution.py:364
  54.0 1.3 %collective-permute-start.12 = (bf16[64,7168]{1,0:T(8,128)(2,1)S(1)}, bf16[64,7168]{1,0:T(8,128)(2,1)}, u32[]{:S(2)}, u32[]{:S(2)}) collective-permute-start(bf16[64,7168]{1,0:T(8,128)(2,1)S(1)} %get-tuple-element.171), channel_id=1, source_target_pairs={{0,32},{8,40},{16,48},{24,56},{32,0},{40,8},{48,16},{56,24},{64,96... | collective-permute-start | bytes 2752520 | tf_op jit(solution)/shard_map/cond/branch_3_fun/ppermute | solution.py:360
  55.3 1.9 %collective-permute-start.13 = (bf16[128,1024]{1,0:T(8,128)(2,1)S(1)}, bf16[128,1024]{1,0:T(8,128)(2,1)S(1)}, u32[]{:S(2)}, u32[]{:S(2)}) collective-permute-start(bf16[128,1024]{1,0:T(8,128)(2,1)S(1)} %get-tuple-element.173), channel_id=1, source_target_pairs={{0,6},{1,7},{2,0},{3,1},{4,2},{5,3},{6,4},{7,5},{8,14},{9,15},{10,... | collective-permute-start | bytes 786440 | tf_op jit(solution)/shard_map/cond/branch_3_fun/ppermute | solution.py:352
  57.2 1.2 %collective-permute-start.15 = (bf16[128,1024]{1,0:T(8,128)(2,1)S(1)}, bf16[128,1024]{1,0:T(8,128)(2,1)S(1)}, u32[]{:S(2)}, u32[]{:S(2)}) collective-permute-start(bf16[128,1024]{1,0:T(8,128)(2,1)S(1)} %get-tuple-element.175), channel_id=1, source_target_pairs={{0,4},{1,5},{2,6},{3,7},{4,0},{5,1},{6,2},{7,3},{8,12},{9,13},{10,... | collective-permute-start | bytes 786440 | tf_op jit(solution)/shard_map/cond/branch_3_fun/ppermute | solution.py:352
  58.4 3.5 %collective-permute-done.13.r1 = bf16[128,1024]{1,0:T(8,128)(2,1)S(1)} collective-permute-done((bf16[128,1024]{1,0:T(8,128)(2,1)S(1)}, bf16[128,1024]{1,0:T(8,128)(2,1)S(1)}, u32[]{:S(2)}, u32[]{:S(2)}) %collective-permute-start.13) | collective-permute-done | bytes 262176 | tf_op jit(solution)/shard_map/cond/branch_3_fun/ppermute | solution.py:352
  61.9 4.0 %collective-permute-done.14.r2 = bf16[128,1024]{1,0:T(8,128)(2,1)S(1)} collective-permute-done((bf16[128,1024]{1,0:T(8,128)(2,1)S(1)}, bf16[128,1024]{1,0:T(8,128)(2,1)S(1)}, u32[]{:S(2)}, u32[]{:S(2)}) %collective-permute-start.14) | collective-permute-done | bytes 262176 | tf_op jit(solution)/shard_map/cond/branch_3_fun/ppermute | solution.py:352
  65.9 3.3 %collective-permute-done.15.r3 = bf16[128,1024]{1,0:T(8,128)(2,1)S(1)} collective-permute-done((bf16[128,1024]{1,0:T(8,128)(2,1)S(1)}, bf16[128,1024]{1,0:T(8,128)(2,1)S(1)}, u32[]{:S(2)}, u32[]{:S(2)}) %collective-permute-start.15) | collective-permute-done | bytes 262176 | tf_op jit(solution)/shard_map/cond/branch_3_fun/ppermute | solution.py:352
  69.1 0.1 keep.18
  69.3 4.9 %collective-permute-done.12 = bf16[64,7168]{1,0:T(8,128)(2,1)} collective-permute-done((bf16[64,7168]{1,0:T(8,128)(2,1)S(1)}, bf16[64,7168]{1,0:T(8,128)(2,1)}, u32[]{:S(2)}, u32[]{:S(2)}) %collective-permute-start.12) | collective-permute-done | bytes 917536 | tf_op jit(solution)/shard_map/cond/branch_3_fun/ppermute | solution.py:360
  74.2 2.8 %collective-permute-start.76 = (bf16[64,1024]{1,0:T(8,128)(2,1)S(1)}, bf16[64,1024]{1,0:T(8,128)(2,1)S(1)}, u32[]{:S(2)}, u32[]{:S(2)}) collective-permute-start(bf16[64,1024]{1,0:T(8,128)(2,1)S(1)} %get-tuple-element.341), channel_id=1, source_target_pairs={{0,1},{1,0},{2,3},{3,2},{4,5},{5,4},{6,7},{7,6},{8,9},{9,8},{10,11... | collective-permute-start | bytes 393224 | tf_op jit(solution)/shard_map/ppermute | solution.py:347
  77.0 0.9 %slice.3 = bf16[64,1024]{1,0:T(8,128)(2,1)S(1)} slice(bf16[64,7168]{1,0:T(8,128)(2,1)} %get-tuple-element.339.new.new_own), slice={[0:64], [6144:7168]} | slice | bytes 262144 | tf_op jit(solution)/shard_map/slice | solution.py:391
  77.9 0.1 collective-permute-start.77
  78.0 2.2 %place_q.1 = bf16[2,64,5120]{2,1,0:T(8,128)(2,1)} custom-call(s32[1]{0:T(128)} %bitcast.pos, s32[1]{0:T(128)S(6)} %copy.55.slot, bf16[64,2560]{1,0:T(8,128)(2,1)S(1)} %get-tuple-element.327.kept_own, bf16[64,2560]{1,0:T(8,128)(2,1)S(1)} %collective-permute-done.75.kept_other, bf16[64,7168]{1,0:T(8,128)(2,1)} %get-tuple-element.339.new.new_own), custom_call_target="tpu_custom_call" | custom-call | bytes 3145728 | tf_op jit(solution)/shard_map/place_q/pallas_call | solution.py:291
  80.2 1.8 %place_kv.1 = (bf16[2,64,1024]{2,1,0:T(8,128)(2,1)}, bf16[2,64,1024]{2,1,0:T(8,128)(2,1)}) custom-call(s32[1]{0:T(128)} %bitcast.pos, s32[1]{0:T(128)S(6)} %copy.55.slot, bf16[64,1024]{1,0:T(8,128)(2,1)S(1)} %get-tuple-element.340.kept_own, bf16[64,7168]{1,0:T(8,128)(2,1)} %get-tuple-element.339.new.new_own, ...), custom_call_target="tpu_custom_call" | custom-call | bytes 2097152 | tf_op jit(solution)/shard_map/place_kv/pallas_call | solution.py:326
  (19 shorter events, 0.0 us)
Async XLA Ops:
  0.6 21.9 %copy-start = (bf16[2,64,5120]{2,1,0:T(8,128)(2,1)S(1)}, bf16[2,64,5120]{2,1,0:T(8,128)(2,1)}, u32[]{:S(2)}) copy-start(bf16[2,64,5120]{2,1,0:T(8,128)(2,1)} %qo.1) | copy-start | bytes 3932164
  1.4 1.0 %copy-start.3 = (bf16[2,64,1024]{2,1,0:T(8,128)(2,1)S(1)}, bf16[2,64,1024]{2,1,0:T(8,128)(2,1)}, u32[]{:S(2)}) copy-start(bf16[2,64,1024]{2,1,0:T(8,128)(2,1)} %k.3) | copy-start | bytes 786436
  2.3 0.9 %copy-start.4 = (bf16[2,64,1024]{2,1,0:T(8,128)(2,1)S(1)}, bf16[2,64,1024]{2,1,0:T(8,128)(2,1)}, u32[]{:S(2)}) copy-start(bf16[2,64,1024]{2,1,0:T(8,128)(2,1)} %v.3) | copy-start | bytes 786436
  3.3 0.7 copy-start.5
  4.1 2.8 %collective-permute-start.60 = (bf16[2,80,1024]{2,1,0:T(8,128)(2,1)S(1)}, bf16[2,80,1024]{2,1,0:T(8,128)(2,1)S(1)}, u32[]{:S(2)}, u32[]{:S(2)}) collective-permute-start(bf16[2,80,1024]{2,1,0:T(8,128)(2,1)S(1)} %pack_kv.1), channel_id=1, source_target_pairs={{0,1},{1,0},{2,3},{3,2},{4,5},{5,4},{6,7},{7,6},{8,9},{9,8},{10,11... | collective-permute-start | bytes 983048 | tf_op jit(solution)/shard_map/ppermute | solution.py:347
  6.9 7.1 %collective-permute-start.64 = (bf16[80,1024]{1,0:T(8,128)(2,1)S(1)}, bf16[80,1024]{1,0:T(8,128)(2,1)S(1)}, u32[]{:S(2)}, u32[]{:S(2)}) collective-permute-start(bf16[80,1024]{1,0:T(8,128)(2,1)S(1)} %get-tuple-element.307.refs_1_.refs_8_.refs_4_), channel_id=1, source_target_pairs={{0,6},{1,7},{2,0},{3,1},{4,2},{5,3},{6,4},{7,5},{8,14},{9,15},{10,... | collective-permute-start | bytes 491528 | tf_op jit(solution)/shard_map/ppermute | solution.py:352
  10.8 6.7 %collective-permute-start.61 = (bf16[64,1024]{1,0:T(8,128)(2,1)S(1)}, bf16[64,1024]{1,0:T(8,128)(2,1)S(1)}, u32[]{:S(2)}, u32[]{:S(2)}) collective-permute-start(bf16[64,1024]{1,0:T(8,128)(2,1)S(1)} %get-tuple-element.306.refs_0_), channel_id=1, source_target_pairs={{0,2},{1,3},{2,4},{3,5},{4,6},{5,7},{6,0},{7,1},{8,10},{9,11},{10,... | collective-permute-start | bytes 393224 | tf_op jit(solution)/shard_map/ppermute | solution.py:352
  10.8 11.7 %collective-permute-start.62 = (bf16[80,1024]{1,0:T(8,128)(2,1)S(1)}, bf16[80,1024]{1,0:T(8,128)(2,1)S(1)}, u32[]{:S(2)}, u32[]{:S(2)}) collective-permute-start(bf16[80,1024]{1,0:T(8,128)(2,1)S(1)} %get-tuple-element.307.refs_1_.refs_8_.refs_4_), channel_id=1, source_target_pairs={{0,2},{1,3},{2,4},{3,5},{4,6},{5,7},{6,0},{7,1},{8,10},{9,11},{10,... | collective-permute-start | bytes 491528 | tf_op jit(solution)/shard_map/ppermute | solution.py:352
  14.0 8.5 %collective-permute-start.66 = (bf16[80,1024]{1,0:T(8,128)(2,1)S(1)}, bf16[80,1024]{1,0:T(8,128)(2,1)S(1)}, u32[]{:S(2)}, u32[]{:S(2)}) collective-permute-start(bf16[80,1024]{1,0:T(8,128)(2,1)S(1)} %collective-permute-done.64.refs_5_.refs_10_.refs_6_), channel_id=1, source_target_pairs={{0,6},{1,7},{2,0},{3,1},{4,2},{5,3},{6,4},{7,5},{8,14},{9,15},{10,... | collective-permute-start | bytes 491528 | tf_op jit(solution)/shard_map/ppermute | solution.py:352
  17.4 5.1 %collective-permute-start.63 = (bf16[64,1024]{1,0:T(8,128)(2,1)S(1)}, bf16[64,1024]{1,0:T(8,128)(2,1)S(1)}, u32[]{:S(2)}, u32[]{:S(2)}) collective-permute-start(bf16[64,1024]{1,0:T(8,128)(2,1)S(1)} %get-tuple-element.306.refs_0_), channel_id=1, source_target_pairs={{0,6},{1,7},{2,0},{3,1},{4,2},{5,3},{6,4},{7,5},{8,14},{9,15},{10,... | collective-permute-start | bytes 393224 | tf_op jit(solution)/shard_map/ppermute | solution.py:352
  17.5 5.1 %collective-permute-start.65 = (bf16[64,1024]{1,0:T(8,128)(2,1)S(1)}, bf16[64,1024]{1,0:T(8,128)(2,1)S(1)}, u32[]{:S(2)}, u32[]{:S(2)}) collective-permute-start(bf16[64,1024]{1,0:T(8,128)(2,1)S(1)} %collective-permute-done.61.refs_2_), channel_id=1, source_target_pairs={{0,2},{1,3},{2,4},{3,5},{4,6},{5,7},{6,0},{7,1},{8,10},{9,11},{10,... | collective-permute-start | bytes 393224 | tf_op jit(solution)/shard_map/ppermute | solution.py:352
  22.6 1.3 %copy-start.1 = (bf16[2,64,5120]{2,1,0:T(8,128)(2,1)S(1)}, bf16[2,64,5120]{2,1,0:T(8,128)(2,1)}, u32[]{:S(2)}) copy-start(bf16[2,64,5120]{2,1,0:T(8,128)(2,1)} %co.1) | copy-start | bytes 3932164
  23.9 7.1 %copy-start.2 = (bf16[2,64,5120]{2,1,0:T(8,128)(2,1)S(1)}, bf16[2,64,5120]{2,1,0:T(8,128)(2,1)}, u32[]{:S(2)}) copy-start(bf16[2,64,5120]{2,1,0:T(8,128)(2,1)} %co.1) | copy-start | bytes 3932164
  24.2 6.8 %collective-permute-start.67 = (bf16[2,2,64,2560]{3,2,1,0:T(8,128)(2,1)S(1)}, bf16[2,2,64,2560]{3,2,1,0:T(8,128)(2,1)S(1)}, u32[]{:S(2)}, u32[]{:S(2)}) collective-permute-start(bf16[2,2,64,2560]{3,2,1,0:T(8,128)(2,1)S(1)} %pack_q.1), channel_id=1, source_target_pairs={{0,1},{1,0},{2,3},{3,2},{4,5},{5,4},{6,7},{7,6},{8,9},{9,8},{10,11... | collective-permute-start | bytes 3932168 | tf_op jit(solution)/shard_map/ppermute | solution.py:347
  26.9 13.0 %collective-permute-start.71 = (bf16[128,1024]{1,0:T(8,128)(2,1)S(1)}, bf16[128,1024]{1,0:T(8,128)(2,1)S(1)}, u32[]{:S(2)}, u32[]{:S(2)}) collective-permute-start(bf16[128,1024]{1,0:T(8,128)(2,1)S(1)} %get-tuple-element.322.refs_0_), channel_id=1, source_target_pairs={{0,2},{1,3},{2,4},{3,5},{4,6},{5,7},{6,0},{7,1},{8,10},{9,11},{10,... | collective-permute-start | bytes 786440 | tf_op jit(solution)/shard_map/ppermute | solution.py:352
  27.3 14.4 %collective-permute-start.72 = (bf16[128,1024]{1,0:T(8,128)(2,1)S(1)}, bf16[128,1024]{1,0:T(8,128)(2,1)S(1)}, u32[]{:S(2)}, u32[]{:S(2)}) collective-permute-start(bf16[128,1024]{1,0:T(8,128)(2,1)S(1)} %get-tuple-element.322.refs_0_), channel_id=1, source_target_pairs={{0,6},{1,7},{2,0},{3,1},{4,2},{5,3},{6,4},{7,5},{8,14},{9,15},{10,... | collective-permute-start | bytes 786440 | tf_op jit(solution)/shard_map/ppermute | solution.py:352
  29.8 13.2 %collective-permute-start.73 = (bf16[128,1024]{1,0:T(8,128)(2,1)S(1)}, bf16[128,1024]{1,0:T(8,128)(2,1)S(1)}, u32[]{:S(2)}, u32[]{:S(2)}) collective-permute-start(bf16[128,1024]{1,0:T(8,128)(2,1)S(1)} %get-tuple-element.322.refs_0_), channel_id=1, source_target_pairs={{0,4},{1,5},{2,6},{3,7},{4,0},{5,1},{6,2},{7,3},{8,12},{9,13},{10,... | collective-permute-start | bytes 786440 | tf_op jit(solution)/shard_map/ppermute | solution.py:352
  38.4 13.9 %collective-permute-start.68 = (bf16[128,1024]{1,0:T(8,128)(2,1)S(1)}, bf16[128,1024]{1,0:T(8,128)(2,1)S(1)}, u32[]{:S(2)}, u32[]{:S(2)}) collective-permute-start(bf16[128,1024]{1,0:T(8,128)(2,1)S(1)} %get-tuple-element.315), channel_id=1, source_target_pairs={{0,6},{1,7},{2,0},{3,1},{4,2},{5,3},{6,4},{7,5},{8,14},{9,15},{10,... | collective-permute-start | bytes 786440 | tf_op jit(solution)/shard_map/ppermute | solution.py:352
  39.9 12.4 %collective-permute-start.69 = (bf16[128,1024]{1,0:T(8,128)(2,1)S(1)}, bf16[128,1024]{1,0:T(8,128)(2,1)S(1)}, u32[]{:S(2)}, u32[]{:S(2)}) collective-permute-start(bf16[128,1024]{1,0:T(8,128)(2,1)S(1)} %get-tuple-element.316), channel_id=1, source_target_pairs={{0,2},{1,3},{2,4},{3,5},{4,6},{5,7},{6,0},{7,1},{8,10},{9,11},{10,... | collective-permute-start | bytes 786440 | tf_op jit(solution)/shard_map/ppermute | solution.py:352
  40.0 13.7 %collective-permute-start.70 = (bf16[128,1024]{1,0:T(8,128)(2,1)S(1)}, bf16[128,1024]{1,0:T(8,128)(2,1)S(1)}, u32[]{:S(2)}, u32[]{:S(2)}) collective-permute-start(bf16[128,1024]{1,0:T(8,128)(2,1)S(1)} %get-tuple-element.317), channel_id=1, source_target_pairs={{0,4},{1,5},{2,6},{3,7},{4,0},{5,1},{6,2},{7,3},{8,12},{9,13},{10,... | collective-permute-start | bytes 786440 | tf_op jit(solution)/shard_map/ppermute | solution.py:352
  43.0 10.7 %collective-permute-start.74 = (bf16[64,2560]{1,0:T(8,128)(2,1)S(1)}, bf16[64,2560]{1,0:T(8,128)(2,1)S(1)}, u32[]{:S(2)}, u32[]{:S(2)}) collective-permute-start(bf16[64,2560]{1,0:T(8,128)(2,1)S(1)} %get-tuple-element.321), channel_id=1, source_target_pairs={{0,1},{1,0},{2,3},{3,2},{4,5},{5,4},{6,7},{7,6},{8,9},{9,8},{10,11... | collective-permute-start | bytes 983048 | tf_op jit(solution)/shard_map/ppermute | solution.py:347
  51.6 26.4 %collective-permute-start.75 = (bf16[64,2560]{1,0:T(8,128)(2,1)S(1)}, bf16[64,2560]{1,0:T(8,128)(2,1)S(1)}, u32[]{:S(2)}, u32[]{:S(2)}) collective-permute-start(bf16[64,2560]{1,0:T(8,128)(2,1)S(1)} %get-tuple-element.328), channel_id=1, source_target_pairs={{0,1},{1,0},{2,3},{3,2},{4,5},{5,4},{6,7},{7,6},{8,9},{9,8},{10,11... | collective-permute-start | bytes 983048 | tf_op jit(solution)/shard_map/ppermute | solution.py:347
  54.0 20.2 %collective-permute-start.12 = (bf16[64,7168]{1,0:T(8,128)(2,1)S(1)}, bf16[64,7168]{1,0:T(8,128)(2,1)}, u32[]{:S(2)}, u32[]{:S(2)}) collective-permute-start(bf16[64,7168]{1,0:T(8,128)(2,1)S(1)} %get-tuple-element.171), channel_id=1, source_target_pairs={{0,32},{8,40},{16,48},{24,56},{32,0},{40,8},{48,16},{56,24},{64,96... | collective-permute-start | bytes 2752520 | tf_op jit(solution)/shard_map/cond/branch_3_fun/ppermute | solution.py:360
  55.3 6.6 %collective-permute-start.13 = (bf16[128,1024]{1,0:T(8,128)(2,1)S(1)}, bf16[128,1024]{1,0:T(8,128)(2,1)S(1)}, u32[]{:S(2)}, u32[]{:S(2)}) collective-permute-start(bf16[128,1024]{1,0:T(8,128)(2,1)S(1)} %get-tuple-element.173), channel_id=1, source_target_pairs={{0,6},{1,7},{2,0},{3,1},{4,2},{5,3},{6,4},{7,5},{8,14},{9,15},{10,... | collective-permute-start | bytes 786440 | tf_op jit(solution)/shard_map/cond/branch_3_fun/ppermute | solution.py:352
  57.2 8.7 %collective-permute-start.14 = (bf16[128,1024]{1,0:T(8,128)(2,1)S(1)}, bf16[128,1024]{1,0:T(8,128)(2,1)S(1)}, u32[]{:S(2)}, u32[]{:S(2)}) collective-permute-start(bf16[128,1024]{1,0:T(8,128)(2,1)S(1)} %get-tuple-element.174), channel_id=1, source_target_pairs={{0,2},{1,3},{2,4},{3,5},{4,6},{5,7},{6,0},{7,1},{8,10},{9,11},{10,... | collective-permute-start | bytes 786440 | tf_op jit(solution)/shard_map/cond/branch_3_fun/ppermute | solution.py:352
  57.2 11.9 %collective-permute-start.15 = (bf16[128,1024]{1,0:T(8,128)(2,1)S(1)}, bf16[128,1024]{1,0:T(8,128)(2,1)S(1)}, u32[]{:S(2)}, u32[]{:S(2)}) collective-permute-start(bf16[128,1024]{1,0:T(8,128)(2,1)S(1)} %get-tuple-element.175), channel_id=1, source_target_pairs={{0,4},{1,5},{2,6},{3,7},{4,0},{5,1},{6,2},{7,3},{8,12},{9,13},{10,... | collective-permute-start | bytes 786440 | tf_op jit(solution)/shard_map/cond/branch_3_fun/ppermute | solution.py:352
  74.2 6.0 %collective-permute-start.76 = (bf16[64,1024]{1,0:T(8,128)(2,1)S(1)}, bf16[64,1024]{1,0:T(8,128)(2,1)S(1)}, u32[]{:S(2)}, u32[]{:S(2)}) collective-permute-start(bf16[64,1024]{1,0:T(8,128)(2,1)S(1)} %get-tuple-element.341), channel_id=1, source_target_pairs={{0,1},{1,0},{2,3},{3,2},{4,5},{5,4},{6,7},{7,6},{8,9},{9,8},{10,11... | collective-permute-start | bytes 393224 | tf_op jit(solution)/shard_map/ppermute | solution.py:347
  77.9 2.3 %collective-permute-start.77 = (bf16[64,1024]{1,0:T(8,128)(2,1)S(1)}, bf16[64,1024]{1,0:T(8,128)(2,1)S(1)}, u32[]{:S(2)}, u32[]{:S(2)}) collective-permute-start(bf16[64,1024]{1,0:T(8,128)(2,1)S(1)} %slice.3), channel_id=1, source_target_pairs={{0,1},{1,0},{2,3},{3,2},{4,5},{5,4},{6,7},{7,6},{8,9},{9,8},{10,11... | collective-permute-start | bytes 393224 | tf_op jit(solution)/shard_map/ppermute | solution.py:347

commit v3 on v2

--- a/solution.py
+++ b/solution.py
@@ -21,11 +21,12 @@
 KW = LOCAL_KV * DH
 KVW = 2 * KW
 ROWS_Q = GROUPS * CHUNK
+PAIR = 2
 SCALE = 1.0 / math.sqrt(DH)
 SCALE2 = SCALE * math.log2(math.e)
 BF = jnp.bfloat16
 F32 = jnp.float32
-VMEM_LIMIT = 16 * 1024 * 1024
+VMEM_LIMIT = 24 * 1024 * 1024
 ORDER = (0, 1, 3, 2)
 SMALL_LIMIT = 8 * 1024 * 1024
 
@@ -159,65 +160,68 @@
             allowed = (key_id == query_id) & (key_pos <= query_pos)
             bias[at * CHUNK : (at + 1) * CHUNK, :] = jnp.where(allowed, 0.0, -1e30).astype(F32)
 
-    kv = [piece[...] for piece in pieces]
-    keys = jnp.concatenate([x[:, :DH] for x in kv], axis=0)
-    values = jnp.concatenate([x[:, DH:] for x in kv], axis=0)
-
-    def heads(own, other):
-        parts = []
+    for u in range(PAIR):
+        wide, narrow = u * GROUPS * DH, u * 2 * DH
+        cols = slice(wide, wide + GROUPS * DH)
+        kv = [piece[:, narrow : narrow + 2 * DH] for piece in pieces]
+        keys = jnp.concatenate([x[:, :DH] for x in kv], axis=0)
+        values = jnp.concatenate([x[:, DH:] for x in kv], axis=0)
+
+        def heads(own, other):
+            parts = []
+            for h in range(GROUPS):
+                parts.append(own[:, h * DH : (h + 1) * DH])
+                parts.append(other[:, h * DH : (h + 1) * DH])
+            return jnp.concatenate(parts, axis=0)
+
+        queries = heads(qo[0, :, cols], qx[0, 0, :, cols])
+        cots = heads(co[0, :, cols], qx[0, 1, :, cols])
+        last = (((1,), (1,)), ((), ()))
+        st[u] = lax.dot_general(keys, queries, last, preferred_element_type=F32)
+        dt[u] = lax.dot_general(values, cots, last, preferred_element_type=F32)
         for h in range(GROUPS):
-            parts.append(own[:, h * DH : (h + 1) * DH])
-            parts.append(other[:, h * DH : (h + 1) * DH])
-        return jnp.concatenate(parts, axis=0)
-
-    queries = heads(qo[0], qx[0, 0])
-    cots = heads(co[0], qx[0, 1])
-    last = (((1,), (1,)), ((), ()))
-    st[...] = lax.dot_general(keys, queries, last, preferred_element_type=F32)
-    dt[...] = lax.dot_general(values, cots, last, preferred_element_type=F32)
-    for h in range(GROUPS):
-        cut = slice(h * CHUNK, (h + 1) * CHUNK)
-        s = st[:, cut] * SCALE2 + bias[...]
-        top = jnp.max(s, axis=0, keepdims=True)
-        e = jnp.exp2(s - top)
-        probs = e * (1.0 / jnp.sum(e, axis=0, keepdims=True))
-        dprobs = dt[:, cut]
-        delta = jnp.sum(probs * dprobs, axis=0, keepdims=True)
-        pt[:, cut] = probs.astype(BF)
-        ds[:, cut] = (probs * (dprobs - delta)).astype(BF)
-    grad_k = jnp.dot(ds[...], queries, preferred_element_type=F32) * SCALE
-    grad_v = jnp.dot(pt[...], cots, preferred_element_type=F32)
-    for d, p in enumerate((p0, p1, p2, p3)):
-        cut = slice(d * CHUNK, (d + 1) * CHUNK)
-        p[:, :DH] = grad_k[cut].astype(p.dtype)
-        p[:, DH:] = grad_v[cut].astype(p.dtype)
-    gq_t = jnp.dot(keys.T, ds[...], preferred_element_type=F32) * SCALE
-    for h in range(GROUPS):
-        gq = gq_t[:, h * CHUNK : (h + 1) * CHUNK].T.astype(BF)
-        gqo[:, h * DH : (h + 1) * DH] = gq[:TOK]
-        gqx[:, h * DH : (h + 1) * DH] = gq[TOK:]
+            cut = slice(h * CHUNK, (h + 1) * CHUNK)
+            s = st[u, :, cut] * SCALE2 + bias[...]
+            top = jnp.max(s, axis=0, keepdims=True)
+            e = jnp.exp2(s - top)
+            probs = e * (1.0 / jnp.sum(e, axis=0, keepdims=True))
+            dprobs = dt[u, :, cut]
+            delta = jnp.sum(probs * dprobs, axis=0, keepdims=True)
+            pt[u, :, cut] = probs.astype(BF)
+            ds[u, :, cut] = (probs * (dprobs - delta)).astype(BF)
+        grad_k = jnp.dot(ds[u], queries, preferred_element_type=F32) * SCALE
+        grad_v = jnp.dot(pt[u], cots, preferred_element_type=F32)
+        for d, p in enumerate((p0, p1, p2, p3)):
+            cut = slice(d * CHUNK, (d + 1) * CHUNK)
+            p[:, narrow : narrow + DH] = grad_k[cut].astype(p.dtype)
+            p[:, narrow + DH : narrow + 2 * DH] = grad_v[cut].astype(p.dtype)
+        gq_t = jnp.dot(keys.T, ds[u], preferred_element_type=F32) * SCALE
+        for h in range(GROUPS):
+            gq = gq_t[:, h * CHUNK : (h + 1) * CHUNK].T.astype(BF)
+            gqo[:, wide + h * DH : wide + (h + 1) * DH] = gq[:TOK]
+            gqx[:, wide + h * DH : wide + (h + 1) * DH] = gq[TOK:]
 
 
 def attention(where, which, queries, cotangent, q_other, chunks, id_chunks):
-    own = pl.BlockSpec((1, TOK, GROUPS * DH), lambda g, p, s: (span_of(s, which), 0, core_of(p) * LOCAL_KV + g))
-    other = pl.BlockSpec((1, 2, TOK, GROUPS * DH), lambda g, p, s: (which, 0, 0, g))
-    chunk = pl.BlockSpec((CHUNK, 2 * DH), lambda g, p, s: (0, g))
-    piece = pl.BlockSpec((KEYS // len(chunks), 2 * DH), lambda g, p, s: (0, g))
+    own = pl.BlockSpec((1, TOK, PAIR * GROUPS * DH), lambda g, p, s: (span_of(s, which), 0, core_of(p) * (LOCAL_KV // PAIR) + g))
+    other = pl.BlockSpec((1, 2, TOK, PAIR * GROUPS * DH), lambda g, p, s: (which, 0, 0, g))
+    chunk = pl.BlockSpec((CHUNK, PAIR * 2 * DH), lambda g, p, s: (0, g))
+    piece = pl.BlockSpec((KEYS // len(chunks), PAIR * 2 * DH), lambda g, p, s: (0, g))
     ids = pl.BlockSpec((16, DH), lambda g, p, s: (TOK // 16, which))
-    out_q = pl.BlockSpec((TOK, GROUPS * DH), lambda g, p, s: (0, g))
+    out_q = pl.BlockSpec((TOK, PAIR * GROUPS * DH), lambda g, p, s: (0, g))
     return pl.pallas_call(
         attention_kernel,
         grid_spec=pltpu.PrefetchScalarGridSpec(
             num_scalar_prefetch=2,
-            grid=(LOCAL_KV,),
+            grid=(LOCAL_KV // PAIR,),
             in_specs=[own, own, other] + [piece] * len(chunks) + [ids] * 4,
             out_specs=[out_q, out_q] + [chunk] * 4,
             scratch_shapes=[
                 pltpu.VMEM((KEYS, CHUNK), F32),
-                pltpu.VMEM((KEYS, ROWS_Q), F32),
-                pltpu.VMEM((KEYS, ROWS_Q), F32),
-                pltpu.VMEM((KEYS, ROWS_Q), BF),
-                pltpu.VMEM((KEYS, ROWS_Q), BF),
+                pltpu.VMEM((PAIR, KEYS, ROWS_Q), F32),
+                pltpu.VMEM((PAIR, KEYS, ROWS_Q), F32),
+                pltpu.VMEM((PAIR, KEYS, ROWS_Q), BF),
+                pltpu.VMEM((PAIR, KEYS, ROWS_Q), BF),
             ],
         ),
         out_shape=[jax.ShapeDtypeStruct((TOK, QW), BF)] * 2

time: 83.5 us -> 84.7 us (1.014); the launches traced: 82 us -> 84.8 us
  waiting for transfers between devices: 26.3 us -> 29.8 us
  Pallas kernels: 19.5 us -> 17.8 us
  starting transfers between devices: 29 us -> 30 us
    ppermute x1, starting transfers between devices: 1.28 us -> 3.57 us  [branch(): new = lax.ppermute(handed, 'dp', [(r, r ^ mask) for r in range(replicas)])]
    ppermute x15, waiting for transfers between devices: 20.1 us -> 22.3 us  [ring(): return lax.ppermute(x, 'seq', [(i, (i + 2 * d) % n) for i in range(n)])]
    pallas_call x2, Pallas kernels: 14.8 us -> 13.1 us  [attention(): pl.pallas_call(attention_kernel, grid_spec=pltpu.PrefetchScalarGridSpec(n...]
    ppermute x1, waiting for transfers between devices: 4.9 us -> 6.24 us  [branch(): new = lax.ppermute(handed, 'dp', [(r, r ^ mask) for r in range(replicas)])]
  transfers between devices with their start and end apart: 22 -> 22, of which waited for: 9 -> 10; matrix products, arithmetic and copies ran while one was open for 1% -> 1% of each run, Pallas kernels for 21% -> 18%
where the time goes in v3:
time: 84.7 us; the launch traced here: 84.8 us
  starting transfers between devices  30 us (35%)
  waiting for transfers between devices  29.8 us (35%)
  Pallas kernels  17.8 us (21%)
  local copies, waits for them, and re-layouts  4.8 us (6%)
  between operations  2.16 us (3%)
    ppermute x15, waiting for transfers between devices, ring(): return lax.ppermute(x, 'seq', [(i, (i + 2 * d) % n) for i in range(n)])  22.3 us
    ppermute x15, starting transfers between devices, ring(): return lax.ppermute(x, 'seq', [(i, (i + 2 * d) % n) for i in range(n)])  18.7 us
    pallas_call x2, Pallas kernels, attention(): pl.pallas_call(attention_kernel, grid_spec=pltpu.PrefetchScalarGridSpec(n...  13.1 us
    ppermute x6, starting transfers between devices, core_swap(): return lax.ppermute(x, 'seq', [(i, i ^ 1) for i in range(2 * CHIPS)])  7.7 us
    ppermute x1, waiting for transfers between devices, branch(): new = lax.ppermute(handed, 'dp', [(r, r ^ mask) for r in range(replicas)])  6.24 us
    unnamed x12, local copies, waits for them, and re-layouts  3.89 us
    ppermute x1, starting transfers between devices, branch(): new = lax.ppermute(handed, 'dp', [(r, r ^ mask) for r in range(replicas)])  3.57 us
    pallas_call x1, Pallas kernels, place_q(): pl.pallas_call(place_q_kernel, grid_spec=pltpu.PrefetchScalarGridSpec(num...  2.23 us
  transfers between devices with their start and end apart: 22, of which 10 were waited for; matrix products, arithmetic and copies ran while one was open for 1% of the time, Pallas kernels for 18%

profile of v3, /device:TPU:1, one launch (start us, length us, event | category | flops | bytes accessed | tf_op | source)
XLA Modules:
  0.0 84.8 jit_solution(12861152879604108862)
XLA Ops:
  1.4 0.9 %copy-done.3 = bf16[2,64,1024]{2,1,0:T(8,128)(2,1)S(1)} copy-done((bf16[2,64,1024]{2,1,0:T(8,128)(2,1)S(1)}, bf16[2,64,1024]{2,1,0:T(8,128)(2,1)}, u32[]{:S(2)}) %copy-start.3) | copy-done | bytes 262168
  2.3 0.9 %copy-done.4 = bf16[2,64,1024]{2,1,0:T(8,128)(2,1)S(1)} copy-done((bf16[2,64,1024]{2,1,0:T(8,128)(2,1)S(1)}, bf16[2,64,1024]{2,1,0:T(8,128)(2,1)}, u32[]{:S(2)}) %copy-start.4) | copy-done | bytes 262168
  3.3 0.7 copy-done.5
  4.0 0.1 pack_kv.1
  4.1 1.5 %collective-permute-start.60 = (bf16[2,80,1024]{2,1,0:T(8,128)(2,1)S(1)}, bf16[2,80,1024]{2,1,0:T(8,128)(2,1)S(1)}, u32[]{:S(2)}, u32[]{:S(2)}) collective-permute-start(bf16[2,80,1024]{2,1,0:T(8,128)(2,1)S(1)} %pack_kv.1), channel_id=1, source_target_pairs={{0,1},{1,0},{2,3},{3,2},{4,5},{5,4},{6,7},{7,6},{8,9},{9,8},{10,11... | collective-permute-start | bytes 983048 | tf_op jit(solution)/shard_map/ppermute | solution.py:351
  5.6 1.3 %collective-permute-done.60.got = bf16[2,80,1024]{2,1,0:T(8,128)(2,1)S(1)} collective-permute-done((bf16[2,80,1024]{2,1,0:T(8,128)(2,1)S(1)}, bf16[2,80,1024]{2,1,0:T(8,128)(2,1)S(1)}, u32[]{:S(2)}, u32[]{:S(2)}) %collective-permute-start.60) | collective-permute-done | bytes 327712 | tf_op jit(solution)/shard_map/ppermute | solution.py:351
  6.8 0.1 make_chunks.1
  6.9 3.9 %collective-permute-start.64 = (bf16[80,1024]{1,0:T(8,128)(2,1)S(1)}, bf16[80,1024]{1,0:T(8,128)(2,1)S(1)}, u32[]{:S(2)}, u32[]{:S(2)}) collective-permute-start(bf16[80,1024]{1,0:T(8,128)(2,1)S(1)} %get-tuple-element.307.refs_1_.refs_8_.refs_4_), channel_id=1, source_target_pairs={{0,6},{1,7},{2,0},{3,1},{4,2},{5,3},{6,4},{7,5},{8,14},{9,15},{10,... | collective-permute-start | bytes 491528 | tf_op jit(solution)/shard_map/ppermute | solution.py:356
  10.8 0.0 collective-permute-start.61
  10.8 0.0 collective-permute-start.62
  10.8 3.2 %collective-permute-done.64.refs_5_.refs_10_.refs_6_ = bf16[80,1024]{1,0:T(8,128)(2,1)S(1)} collective-permute-done((bf16[80,1024]{1,0:T(8,128)(2,1)S(1)}, bf16[80,1024]{1,0:T(8,128)(2,1)S(1)}, u32[]{:S(2)}, u32[]{:S(2)}) %collective-permute-start.64) | collective-permute-done | bytes 163872 | tf_op jit(solution)/shard_map/ppermute | solution.py:356
  14.0 3.4 %collective-permute-start.66 = (bf16[80,1024]{1,0:T(8,128)(2,1)S(1)}, bf16[80,1024]{1,0:T(8,128)(2,1)S(1)}, u32[]{:S(2)}, u32[]{:S(2)}) collective-permute-start(bf16[80,1024]{1,0:T(8,128)(2,1)S(1)} %collective-permute-done.64.refs_5_.refs_10_.refs_6_), channel_id=1, source_target_pairs={{0,6},{1,7},{2,0},{3,1},{4,2},{5,3},{6,4},{7,5},{8,14},{9,15},{10,... | collective-permute-start | bytes 491528 | tf_op jit(solution)/shard_map/ppermute | solution.py:356
  17.4 0.0 collective-permute-start.63
  17.5 1.4 %collective-permute-start.65 = (bf16[64,1024]{1,0:T(8,128)(2,1)S(1)}, bf16[64,1024]{1,0:T(8,128)(2,1)S(1)}, u32[]{:S(2)}, u32[]{:S(2)}) collective-permute-start(bf16[64,1024]{1,0:T(8,128)(2,1)S(1)} %collective-permute-done.61.refs_2_), channel_id=1, source_target_pairs={{0,2},{1,3},{2,4},{3,5},{4,6},{5,7},{6,0},{7,1},{8,10},{9,11},{10,... | collective-permute-start | bytes 393224 | tf_op jit(solution)/shard_map/ppermute | solution.py:356
  18.9 3.6 %collective-permute-done.63.refs_4_ = bf16[64,1024]{1,0:T(8,128)(2,1)S(1)} collective-permute-done((bf16[64,1024]{1,0:T(8,128)(2,1)S(1)}, bf16[64,1024]{1,0:T(8,128)(2,1)S(1)}, u32[]{:S(2)}, u32[]{:S(2)}) %collective-permute-start.63) | collective-permute-done | bytes 131104 | tf_op jit(solution)/shard_map/ppermute | solution.py:356
  22.6 0.0 copy-start.1
  22.6 1.3 %copy-done.1 = bf16[2,64,5120]{2,1,0:T(8,128)(2,1)S(1)} copy-done((bf16[2,64,5120]{2,1,0:T(8,128)(2,1)S(1)}, bf16[2,64,5120]{2,1,0:T(8,128)(2,1)}, u32[]{:S(2)}) %copy-start.1) | copy-done | bytes 1310744
  23.9 0.3 pack_q.1
  24.2 2.8 %collective-permute-start.67 = (bf16[2,2,64,2560]{3,2,1,0:T(8,128)(2,1)S(1)}, bf16[2,2,64,2560]{3,2,1,0:T(8,128)(2,1)S(1)}, u32[]{:S(2)}, u32[]{:S(2)}) collective-permute-start(bf16[2,2,64,2560]{3,2,1,0:T(8,128)(2,1)S(1)} %pack_q.1), channel_id=1, source_target_pairs={{0,1},{1,0},{2,3},{3,2},{4,5},{5,4},{6,7},{7,6},{8,9},{9,8},{10,11... | collective-permute-start | bytes 3932168 | tf_op jit(solution)/shard_map/ppermute | solution.py:351
  26.9 0.4 collective-permute-start.71
  27.3 2.4 %collective-permute-start.72 = (bf16[128,1024]{1,0:T(8,128)(2,1)S(1)}, bf16[128,1024]{1,0:T(8,128)(2,1)S(1)}, u32[]{:S(2)}, u32[]{:S(2)}) collective-permute-start(bf16[128,1024]{1,0:T(8,128)(2,1)S(1)} %get-tuple-element.322.refs_0_), channel_id=1, source_target_pairs={{0,6},{1,7},{2,0},{3,1},{4,2},{5,3},{6,4},{7,5},{8,14},{9,15},{10,... | collective-permute-start | bytes 786440 | tf_op jit(solution)/shard_map/ppermute | solution.py:356
  29.8 1.2 %collective-permute-start.73 = (bf16[128,1024]{1,0:T(8,128)(2,1)S(1)}, bf16[128,1024]{1,0:T(8,128)(2,1)S(1)}, u32[]{:S(2)}, u32[]{:S(2)}) collective-permute-start(bf16[128,1024]{1,0:T(8,128)(2,1)S(1)} %get-tuple-element.322.refs_0_), channel_id=1, source_target_pairs={{0,4},{1,5},{2,6},{3,7},{4,0},{5,1},{6,2},{7,3},{8,12},{9,13},{10,... | collective-permute-start | bytes 786440 | tf_op jit(solution)/shard_map/ppermute | solution.py:356
  31.0 6.6 %attention.2 = (bf16[64,2560]{1,0:T(8,128)(2,1)S(1)}, bf16[64,2560]{1,0:T(8,128)(2,1)S(1)}, f32[128,1024]{1,0:T(8,128)S(1)}, bf16[128,1024]{1,0:T(8,128)(2,1)S(1...) custom-call(s32[1]{0:T(128)} %bitcast.pos, s32[1]{0:T(128)S(6)} %copy.55.slot, ...), custom_call_target="tpu_custom_call" | custom-call | flops 1677721600 | bytes 5242880 | tf_op jit(solution)/shard_map/attention/pallas_call | solution.py:212
  37.5 1.5 %collective-permute-start.68 = (bf16[128,1024]{1,0:T(8,128)(2,1)S(1)}, bf16[128,1024]{1,0:T(8,128)(2,1)S(1)}, u32[]{:S(2)}, u32[]{:S(2)}) collective-permute-start(bf16[128,1024]{1,0:T(8,128)(2,1)S(1)} %get-tuple-element.315), channel_id=1, source_target_pairs={{0,6},{1,7},{2,0},{3,1},{4,2},{5,3},{6,4},{7,5},{8,14},{9,15},{10,... | collective-permute-start | bytes 786440 | tf_op jit(solution)/shard_map/ppermute | solution.py:356
  39.1 0.0 collective-permute-start.69
  39.1 1.8 %collective-permute-start.70 = (bf16[128,1024]{1,0:T(8,128)(2,1)S(1)}, bf16[128,1024]{1,0:T(8,128)(2,1)S(1)}, u32[]{:S(2)}, u32[]{:S(2)}) collective-permute-start(bf16[128,1024]{1,0:T(8,128)(2,1)S(1)} %get-tuple-element.317), channel_id=1, source_target_pairs={{0,4},{1,5},{2,6},{3,7},{4,0},{5,1},{6,2},{7,3},{8,12},{9,13},{10,... | collective-permute-start | bytes 786440 | tf_op jit(solution)/shard_map/ppermute | solution.py:356
  40.9 2.1 %collective-permute-done.73.refs_3_ = bf16[128,1024]{1,0:T(8,128)(2,1)S(1)} collective-permute-done((bf16[128,1024]{1,0:T(8,128)(2,1)S(1)}, bf16[128,1024]{1,0:T(8,128)(2,1)S(1)}, u32[]{:S(2)}, u32[]{:S(2)}) %collective-permute-start.73) | collective-permute-done | bytes 262176 | tf_op jit(solution)/shard_map/ppermute | solution.py:356
  43.0 1.3 %collective-permute-start.74 = (bf16[64,2560]{1,0:T(8,128)(2,1)S(1)}, bf16[64,2560]{1,0:T(8,128)(2,1)S(1)}, u32[]{:S(2)}, u32[]{:S(2)}) collective-permute-start(bf16[64,2560]{1,0:T(8,128)(2,1)S(1)} %get-tuple-element.321), channel_id=1, source_target_pairs={{0,1},{1,0},{2,3},{3,2},{4,5},{5,4},{6,7},{7,6},{8,9},{9,8},{10,11... | collective-permute-start | bytes 983048 | tf_op jit(solution)/shard_map/ppermute | solution.py:351
  44.3 6.5 %attention.3 = (bf16[64,2560]{1,0:T(8,128)(2,1)S(1)}, bf16[64,2560]{1,0:T(8,128)(2,1)S(1)}, f32[128,1024]{1,0:T(8,128)S(1)}, bf16[128,1024]{1,0:T(8,128)(2,1)S(1...) custom-call(s32[1]{0:T(128)} %bitcast.pos, s32[1]{0:T(128)S(6)} %copy.55.slot, ...), custom_call_target="tpu_custom_call" | custom-call | flops 1677721600 | bytes 5242880 | tf_op jit(solution)/shard_map/attention/pallas_call | solution.py:212
  50.8 0.3 collective-permute-start.75
  51.7 0.3 collective-permute-done.68.r1
  52.0 2.2 %collective-permute-done.70.r3 = bf16[128,1024]{1,0:T(8,128)(2,1)S(1)} collective-permute-done((bf16[128,1024]{1,0:T(8,128)(2,1)S(1)}, bf16[128,1024]{1,0:T(8,128)(2,1)S(1)}, u32[]{:S(2)}, u32[]{:S(2)}) %collective-permute-start.70) | collective-permute-done | bytes 262176 | tf_op jit(solution)/shard_map/ppermute | solution.py:356
  54.2 0.2 hand_over.1
  54.4 23.6 %conditional.1 = (bf16[64,7168]{1,0:T(8,128)(2,1)}, bf16[64,1024]{1,0:T(8,128)(2,1)S(1)}, bf16[64,1024]{1,0:T(8,128)(2,1)S(1)}) conditional(s32[]{:T(128)} %bitcast.1, (bf16[64,7168]{1,0:T(8,128)(2,1)S(1)}, bf16[128,1024]{1,0:T(8,128)(2,1)S(1)}, bf16[128,1024]{1,0:T(8,128)(2,1)S(1)}, bf16[128,1024]{1,0:T(8,128)(2,1)S(1)}, ...), branch_computations={%region_0.0_spmd, %region_1.0_spmd, %region_2.0_spmd, %region_3.0_... | conditional | bytes 8913080 | solution.py:368
  54.7 3.6 %collective-permute-start.48 = (bf16[64,7168]{1,0:T(8,128)(2,1)S(1)}, bf16[64,7168]{1,0:T(8,128)(2,1)}, u32[]{:S(2)}, u32[]{:S(2)}) collective-permute-start(bf16[64,7168]{1,0:T(8,128)(2,1)S(1)} %get-tuple-element.234), channel_id=1, source_target_pairs={{0,104},{8,96},{16,120},{24,112},{32,72},{40,64},{48,88},{56,80},{... | collective-permute-start | bytes 2752520 | tf_op jit(solution)/shard_map/cond/branch_12_fun/ppermute | solution.py:364
  58.3 1.4 %collective-permute-start.49 = (bf16[128,1024]{1,0:T(8,128)(2,1)S(1)}, bf16[128,1024]{1,0:T(8,128)(2,1)S(1)}, u32[]{:S(2)}, u32[]{:S(2)}) collective-permute-start(bf16[128,1024]{1,0:T(8,128)(2,1)S(1)} %get-tuple-element.236), channel_id=1, source_target_pairs={{0,6},{1,7},{2,0},{3,1},{4,2},{5,3},{6,4},{7,5},{8,14},{9,15},{10,... | collective-permute-start | bytes 786440 | tf_op jit(solution)/shard_map/cond/branch_12_fun/ppermute | solution.py:356
  59.6 0.1 collective-permute-start.50
  59.7 1.1 %collective-permute-start.51 = (bf16[128,1024]{1,0:T(8,128)(2,1)S(1)}, bf16[128,1024]{1,0:T(8,128)(2,1)S(1)}, u32[]{:S(2)}, u32[]{:S(2)}) collective-permute-start(bf16[128,1024]{1,0:T(8,128)(2,1)S(1)} %get-tuple-element.238), channel_id=1, source_target_pairs={{0,4},{1,5},{2,6},{3,7},{4,0},{5,1},{6,2},{7,3},{8,12},{9,13},{10,... | collective-permute-start | bytes 786440 | tf_op jit(solution)/shard_map/cond/branch_12_fun/ppermute | solution.py:356
  60.8 4.2 %collective-permute-done.49.r1 = bf16[128,1024]{1,0:T(8,128)(2,1)S(1)} collective-permute-done((bf16[128,1024]{1,0:T(8,128)(2,1)S(1)}, bf16[128,1024]{1,0:T(8,128)(2,1)S(1)}, u32[]{:S(2)}, u32[]{:S(2)}) %collective-permute-start.49) | collective-permute-done | bytes 262176 | tf_op jit(solution)/shard_map/cond/branch_12_fun/ppermute | solution.py:356
  65.0 3.4 %collective-permute-done.50.r2 = bf16[128,1024]{1,0:T(8,128)(2,1)S(1)} collective-permute-done((bf16[128,1024]{1,0:T(8,128)(2,1)S(1)}, bf16[128,1024]{1,0:T(8,128)(2,1)S(1)}, u32[]{:S(2)}, u32[]{:S(2)}) %collective-permute-start.50) | collective-permute-done | bytes 262176 | tf_op jit(solution)/shard_map/cond/branch_12_fun/ppermute | solution.py:356
  68.4 3.2 %collective-permute-done.51.r3 = bf16[128,1024]{1,0:T(8,128)(2,1)S(1)} collective-permute-done((bf16[128,1024]{1,0:T(8,128)(2,1)S(1)}, bf16[128,1024]{1,0:T(8,128)(2,1)S(1)}, u32[]{:S(2)}, u32[]{:S(2)}) %collective-permute-start.51) | collective-permute-done | bytes 262176 | tf_op jit(solution)/shard_map/cond/branch_12_fun/ppermute | solution.py:356
  71.6 0.1 keep.27
  71.7 6.2 %collective-permute-done.48 = bf16[64,7168]{1,0:T(8,128)(2,1)} collective-permute-done((bf16[64,7168]{1,0:T(8,128)(2,1)S(1)}, bf16[64,7168]{1,0:T(8,128)(2,1)}, u32[]{:S(2)}, u32[]{:S(2)}) %collective-permute-start.48) | collective-permute-done | bytes 917536 | tf_op jit(solution)/shard_map/cond/branch_12_fun/ppermute | solution.py:364
  78.0 1.8 %collective-permute-start.76 = (bf16[64,1024]{1,0:T(8,128)(2,1)S(1)}, bf16[64,1024]{1,0:T(8,128)(2,1)S(1)}, u32[]{:S(2)}, u32[]{:S(2)}) collective-permute-start(bf16[64,1024]{1,0:T(8,128)(2,1)S(1)} %get-tuple-element.341), channel_id=1, source_target_pairs={{0,1},{1,0},{2,3},{3,2},{4,5},{5,4},{6,7},{7,6},{8,9},{9,8},{10,11... | collective-permute-start | bytes 393224 | tf_op jit(solution)/shard_map/ppermute | solution.py:351
  79.7 0.9 %slice.3 = bf16[64,1024]{1,0:T(8,128)(2,1)S(1)} slice(bf16[64,7168]{1,0:T(8,128)(2,1)} %get-tuple-element.339.new.new_own), slice={[0:64], [6144:7168]} | slice | bytes 262144 | tf_op jit(solution)/shard_map/slice | solution.py:395
  80.7 0.1 collective-permute-start.77
  80.8 2.2 %place_q.1 = bf16[2,64,5120]{2,1,0:T(8,128)(2,1)} custom-call(s32[1]{0:T(128)} %bitcast.pos, s32[1]{0:T(128)S(6)} %copy.55.slot, bf16[64,2560]{1,0:T(8,128)(2,1)S(1)} %get-tuple-element.327.kept_own, bf16[64,2560]{1,0:T(8,128)(2,1)S(1)} %collective-permute-done.75.kept_other, bf16[64,7168]{1,0:T(8,128)(2,1)} %get-tuple-element.339.new.new_own), custom_call_target="tpu_custom_call" | custom-call | bytes 3145728 | tf_op jit(solution)/shard_map/place_q/pallas_call | solution.py:295
  83.0 1.8 %place_kv.1 = (bf16[2,64,1024]{2,1,0:T(8,128)(2,1)}, bf16[2,64,1024]{2,1,0:T(8,128)(2,1)}) custom-call(s32[1]{0:T(128)} %bitcast.pos, s32[1]{0:T(128)S(6)} %copy.55.slot, bf16[64,1024]{1,0:T(8,128)(2,1)S(1)} %get-tuple-element.340.kept_own, bf16[64,7168]{1,0:T(8,128)(2,1)} %get-tuple-element.339.new.new_own, ...), custom_call_target="tpu_custom_call" | custom-call | bytes 2097152 | tf_op jit(solution)/shard_map/place_kv/pallas_call | solution.py:330
  (19 shorter events, 0.0 us)
Async XLA Ops:
  0.6 21.9 %copy-start = (bf16[2,64,5120]{2,1,0:T(8,128)(2,1)S(1)}, bf16[2,64,5120]{2,1,0:T(8,128)(2,1)}, u32[]{:S(2)}) copy-start(bf16[2,64,5120]{2,1,0:T(8,128)(2,1)} %qo.1) | copy-start | bytes 3932164
  1.4 1.0 %copy-start.3 = (bf16[2,64,1024]{2,1,0:T(8,128)(2,1)S(1)}, bf16[2,64,1024]{2,1,0:T(8,128)(2,1)}, u32[]{:S(2)}) copy-start(bf16[2,64,1024]{2,1,0:T(8,128)(2,1)} %k.3) | copy-start | bytes 786436
  2.3 0.9 %copy-start.4 = (bf16[2,64,1024]{2,1,0:T(8,128)(2,1)S(1)}, bf16[2,64,1024]{2,1,0:T(8,128)(2,1)}, u32[]{:S(2)}) copy-start(bf16[2,64,1024]{2,1,0:T(8,128)(2,1)} %v.3) | copy-start | bytes 786436
  3.3 0.7 copy-start.5
  4.1 2.8 %collective-permute-start.60 = (bf16[2,80,1024]{2,1,0:T(8,128)(2,1)S(1)}, bf16[2,80,1024]{2,1,0:T(8,128)(2,1)S(1)}, u32[]{:S(2)}, u32[]{:S(2)}) collective-permute-start(bf16[2,80,1024]{2,1,0:T(8,128)(2,1)S(1)} %pack_kv.1), channel_id=1, source_target_pairs={{0,1},{1,0},{2,3},{3,2},{4,5},{5,4},{6,7},{7,6},{8,9},{9,8},{10,11... | collective-permute-start | bytes 983048 | tf_op jit(solution)/shard_map/ppermute | solution.py:351
  6.9 7.1 %collective-permute-start.64 = (bf16[80,1024]{1,0:T(8,128)(2,1)S(1)}, bf16[80,1024]{1,0:T(8,128)(2,1)S(1)}, u32[]{:S(2)}, u32[]{:S(2)}) collective-permute-start(bf16[80,1024]{1,0:T(8,128)(2,1)S(1)} %get-tuple-element.307.refs_1_.refs_8_.refs_4_), channel_id=1, source_target_pairs={{0,6},{1,7},{2,0},{3,1},{4,2},{5,3},{6,4},{7,5},{8,14},{9,15},{10,... | collective-permute-start | bytes 491528 | tf_op jit(solution)/shard_map/ppermute | solution.py:356
  10.8 6.7 %collective-permute-start.61 = (bf16[64,1024]{1,0:T(8,128)(2,1)S(1)}, bf16[64,1024]{1,0:T(8,128)(2,1)S(1)}, u32[]{:S(2)}, u32[]{:S(2)}) collective-permute-start(bf16[64,1024]{1,0:T(8,128)(2,1)S(1)} %get-tuple-element.306.refs_0_), channel_id=1, source_target_pairs={{0,2},{1,3},{2,4},{3,5},{4,6},{5,7},{6,0},{7,1},{8,10},{9,11},{10,... | collective-permute-start | bytes 393224 | tf_op jit(solution)/shard_map/ppermute | solution.py:356
  10.8 11.7 %collective-permute-start.62 = (bf16[80,1024]{1,0:T(8,128)(2,1)S(1)}, bf16[80,1024]{1,0:T(8,128)(2,1)S(1)}, u32[]{:S(2)}, u32[]{:S(2)}) collective-permute-start(bf16[80,1024]{1,0:T(8,128)(2,1)S(1)} %get-tuple-element.307.refs_1_.refs_8_.refs_4_), channel_id=1, source_target_pairs={{0,2},{1,3},{2,4},{3,5},{4,6},{5,7},{6,0},{7,1},{8,10},{9,11},{10,... | collective-permute-start | bytes 491528 | tf_op jit(solution)/shard_map/ppermute | solution.py:356
  14.0 8.5 %collective-permute-start.66 = (bf16[80,1024]{1,0:T(8,128)(2,1)S(1)}, bf16[80,1024]{1,0:T(8,128)(2,1)S(1)}, u32[]{:S(2)}, u32[]{:S(2)}) collective-permute-start(bf16[80,1024]{1,0:T(8,128)(2,1)S(1)} %collective-permute-done.64.refs_5_.refs_10_.refs_6_), channel_id=1, source_target_pairs={{0,6},{1,7},{2,0},{3,1},{4,2},{5,3},{6,4},{7,5},{8,14},{9,15},{10,... | collective-permute-start | bytes 491528 | tf_op jit(solution)/shard_map/ppermute | solution.py:356
  17.4 5.1 %collective-permute-start.63 = (bf16[64,1024]{1,0:T(8,128)(2,1)S(1)}, bf16[64,1024]{1,0:T(8,128)(2,1)S(1)}, u32[]{:S(2)}, u32[]{:S(2)}) collective-permute-start(bf16[64,1024]{1,0:T(8,128)(2,1)S(1)} %get-tuple-element.306.refs_0_), channel_id=1, source_target_pairs={{0,6},{1,7},{2,0},{3,1},{4,2},{5,3},{6,4},{7,5},{8,14},{9,15},{10,... | collective-permute-start | bytes 393224 | tf_op jit(solution)/shard_map/ppermute | solution.py:356
  17.5 5.1 %collective-permute-start.65 = (bf16[64,1024]{1,0:T(8,128)(2,1)S(1)}, bf16[64,1024]{1,0:T(8,128)(2,1)S(1)}, u32[]{:S(2)}, u32[]{:S(2)}) collective-permute-start(bf16[64,1024]{1,0:T(8,128)(2,1)S(1)} %collective-permute-done.61.refs_2_), channel_id=1, source_target_pairs={{0,2},{1,3},{2,4},{3,5},{4,6},{5,7},{6,0},{7,1},{8,10},{9,11},{10,... | collective-permute-start | bytes 393224 | tf_op jit(solution)/shard_map/ppermute | solution.py:356
  22.6 1.3 %copy-start.1 = (bf16[2,64,5120]{2,1,0:T(8,128)(2,1)S(1)}, bf16[2,64,5120]{2,1,0:T(8,128)(2,1)}, u32[]{:S(2)}) copy-start(bf16[2,64,5120]{2,1,0:T(8,128)(2,1)} %co.1) | copy-start | bytes 3932164
  23.9 7.1 %copy-start.2 = (bf16[2,64,5120]{2,1,0:T(8,128)(2,1)S(1)}, bf16[2,64,5120]{2,1,0:T(8,128)(2,1)}, u32[]{:S(2)}) copy-start(bf16[2,64,5120]{2,1,0:T(8,128)(2,1)} %co.1) | copy-start | bytes 3932164
  24.2 6.8 %collective-permute-start.67 = (bf16[2,2,64,2560]{3,2,1,0:T(8,128)(2,1)S(1)}, bf16[2,2,64,2560]{3,2,1,0:T(8,128)(2,1)S(1)}, u32[]{:S(2)}, u32[]{:S(2)}) collective-permute-start(bf16[2,2,64,2560]{3,2,1,0:T(8,128)(2,1)S(1)} %pack_q.1), channel_id=1, source_target_pairs={{0,1},{1,0},{2,3},{3,2},{4,5},{5,4},{6,7},{7,6},{8,9},{9,8},{10,11... | collective-permute-start | bytes 3932168 | tf_op jit(solution)/shard_map/ppermute | solution.py:351
  26.9 12.2 %collective-permute-start.71 = (bf16[128,1024]{1,0:T(8,128)(2,1)S(1)}, bf16[128,1024]{1,0:T(8,128)(2,1)S(1)}, u32[]{:S(2)}, u32[]{:S(2)}) collective-permute-start(bf16[128,1024]{1,0:T(8,128)(2,1)S(1)} %get-tuple-element.322.refs_0_), channel_id=1, source_target_pairs={{0,2},{1,3},{2,4},{3,5},{4,6},{5,7},{6,0},{7,1},{8,10},{9,11},{10,... | collective-permute-start | bytes 786440 | tf_op jit(solution)/shard_map/ppermute | solution.py:356
  27.3 13.5 %collective-permute-start.72 = (bf16[128,1024]{1,0:T(8,128)(2,1)S(1)}, bf16[128,1024]{1,0:T(8,128)(2,1)S(1)}, u32[]{:S(2)}, u32[]{:S(2)}) collective-permute-start(bf16[128,1024]{1,0:T(8,128)(2,1)S(1)} %get-tuple-element.322.refs_0_), channel_id=1, source_target_pairs={{0,6},{1,7},{2,0},{3,1},{4,2},{5,3},{6,4},{7,5},{8,14},{9,15},{10,... | collective-permute-start | bytes 786440 | tf_op jit(solution)/shard_map/ppermute | solution.py:356
  29.8 13.2 %collective-permute-start.73 = (bf16[128,1024]{1,0:T(8,128)(2,1)S(1)}, bf16[128,1024]{1,0:T(8,128)(2,1)S(1)}, u32[]{:S(2)}, u32[]{:S(2)}) collective-permute-start(bf16[128,1024]{1,0:T(8,128)(2,1)S(1)} %get-tuple-element.322.refs_0_), channel_id=1, source_target_pairs={{0,4},{1,5},{2,6},{3,7},{4,0},{5,1},{6,2},{7,3},{8,12},{9,13},{10,... | collective-permute-start | bytes 786440 | tf_op jit(solution)/shard_map/ppermute | solution.py:356
  37.5 14.5 %collective-permute-start.68 = (bf16[128,1024]{1,0:T(8,128)(2,1)S(1)}, bf16[128,1024]{1,0:T(8,128)(2,1)S(1)}, u32[]{:S(2)}, u32[]{:S(2)}) collective-permute-start(bf16[128,1024]{1,0:T(8,128)(2,1)S(1)} %get-tuple-element.315), channel_id=1, source_target_pairs={{0,6},{1,7},{2,0},{3,1},{4,2},{5,3},{6,4},{7,5},{8,14},{9,15},{10,... | collective-permute-start | bytes 786440 | tf_op jit(solution)/shard_map/ppermute | solution.py:356
  39.1 12.9 %collective-permute-start.69 = (bf16[128,1024]{1,0:T(8,128)(2,1)S(1)}, bf16[128,1024]{1,0:T(8,128)(2,1)S(1)}, u32[]{:S(2)}, u32[]{:S(2)}) collective-permute-start(bf16[128,1024]{1,0:T(8,128)(2,1)S(1)} %get-tuple-element.316), channel_id=1, source_target_pairs={{0,2},{1,3},{2,4},{3,5},{4,6},{5,7},{6,0},{7,1},{8,10},{9,11},{10,... | collective-permute-start | bytes 786440 | tf_op jit(solution)/shard_map/ppermute | solution.py:356
  39.1 15.1 %collective-permute-start.70 = (bf16[128,1024]{1,0:T(8,128)(2,1)S(1)}, bf16[128,1024]{1,0:T(8,128)(2,1)S(1)}, u32[]{:S(2)}, u32[]{:S(2)}) collective-permute-start(bf16[128,1024]{1,0:T(8,128)(2,1)S(1)} %get-tuple-element.317), channel_id=1, source_target_pairs={{0,4},{1,5},{2,6},{3,7},{4,0},{5,1},{6,2},{7,3},{8,12},{9,13},{10,... | collective-permute-start | bytes 786440 | tf_op jit(solution)/shard_map/ppermute | solution.py:356
  43.0 11.2 %collective-permute-start.74 = (bf16[64,2560]{1,0:T(8,128)(2,1)S(1)}, bf16[64,2560]{1,0:T(8,128)(2,1)S(1)}, u32[]{:S(2)}, u32[]{:S(2)}) collective-permute-start(bf16[64,2560]{1,0:T(8,128)(2,1)S(1)} %get-tuple-element.321), channel_id=1, source_target_pairs={{0,1},{1,0},{2,3},{3,2},{4,5},{5,4},{6,7},{7,6},{8,9},{9,8},{10,11... | collective-permute-start | bytes 983048 | tf_op jit(solution)/shard_map/ppermute | solution.py:351
  50.8 29.9 %collective-permute-start.75 = (bf16[64,2560]{1,0:T(8,128)(2,1)S(1)}, bf16[64,2560]{1,0:T(8,128)(2,1)S(1)}, u32[]{:S(2)}, u32[]{:S(2)}) collective-permute-start(bf16[64,2560]{1,0:T(8,128)(2,1)S(1)} %get-tuple-element.328), channel_id=1, source_target_pairs={{0,1},{1,0},{2,3},{3,2},{4,5},{5,4},{6,7},{7,6},{8,9},{9,8},{10,11... | collective-permute-start | bytes 983048 | tf_op jit(solution)/shard_map/ppermute | solution.py:351
  54.7 23.3 %collective-permute-start.48 = (bf16[64,7168]{1,0:T(8,128)(2,1)S(1)}, bf16[64,7168]{1,0:T(8,128)(2,1)}, u32[]{:S(2)}, u32[]{:S(2)}) collective-permute-start(bf16[64,7168]{1,0:T(8,128)(2,1)S(1)} %get-tuple-element.234), channel_id=1, source_target_pairs={{0,104},{8,96},{16,120},{24,112},{32,72},{40,64},{48,88},{56,80},{... | collective-permute-start | bytes 2752520 | tf_op jit(solution)/shard_map/cond/branch_12_fun/ppermute | solution.py:364
  58.3 6.8 %collective-permute-start.49 = (bf16[128,1024]{1,0:T(8,128)(2,1)S(1)}, bf16[128,1024]{1,0:T(8,128)(2,1)S(1)}, u32[]{:S(2)}, u32[]{:S(2)}) collective-permute-start(bf16[128,1024]{1,0:T(8,128)(2,1)S(1)} %get-tuple-element.236), channel_id=1, source_target_pairs={{0,6},{1,7},{2,0},{3,1},{4,2},{5,3},{6,4},{7,5},{8,14},{9,15},{10,... | collective-permute-start | bytes 786440 | tf_op jit(solution)/shard_map/cond/branch_12_fun/ppermute | solution.py:356
  59.6 8.8 %collective-permute-start.50 = (bf16[128,1024]{1,0:T(8,128)(2,1)S(1)}, bf16[128,1024]{1,0:T(8,128)(2,1)S(1)}, u32[]{:S(2)}, u32[]{:S(2)}) collective-permute-start(bf16[128,1024]{1,0:T(8,128)(2,1)S(1)} %get-tuple-element.237), channel_id=1, source_target_pairs={{0,2},{1,3},{2,4},{3,5},{4,6},{5,7},{6,0},{7,1},{8,10},{9,11},{10,... | collective-permute-start | bytes 786440 | tf_op jit(solution)/shard_map/cond/branch_12_fun/ppermute | solution.py:356
  59.7 11.9 %collective-permute-start.51 = (bf16[128,1024]{1,0:T(8,128)(2,1)S(1)}, bf16[128,1024]{1,0:T(8,128)(2,1)S(1)}, u32[]{:S(2)}, u32[]{:S(2)}) collective-permute-start(bf16[128,1024]{1,0:T(8,128)(2,1)S(1)} %get-tuple-element.238), channel_id=1, source_target_pairs={{0,4},{1,5},{2,6},{3,7},{4,0},{5,1},{6,2},{7,3},{8,12},{9,13},{10,... | collective-permute-start | bytes 786440 | tf_op jit(solution)/shard_map/cond/branch_12_fun/ppermute | solution.py:356
  78.0 5.0 %collective-permute-start.76 = (bf16[64,1024]{1,0:T(8,128)(2,1)S(1)}, bf16[64,1024]{1,0:T(8,128)(2,1)S(1)}, u32[]{:S(2)}, u32[]{:S(2)}) collective-permute-start(bf16[64,1024]{1,0:T(8,128)(2,1)S(1)} %get-tuple-element.341), channel_id=1, source_target_pairs={{0,1},{1,0},{2,3},{3,2},{4,5},{5,4},{6,7},{7,6},{8,9},{9,8},{10,11... | collective-permute-start | bytes 393224 | tf_op jit(solution)/shard_map/ppermute | solution.py:351
  80.7 2.3 %collective-permute-start.77 = (bf16[64,1024]{1,0:T(8,128)(2,1)S(1)}, bf16[64,1024]{1,0:T(8,128)(2,1)S(1)}, u32[]{:S(2)}, u32[]{:S(2)}) collective-permute-start(bf16[64,1024]{1,0:T(8,128)(2,1)S(1)} %slice.3), channel_id=1, source_target_pairs={{0,1},{1,0},{2,3},{3,2},{4,5},{5,4},{6,7},{7,6},{8,9},{9,8},{10,11... | collective-permute-start | bytes 393224 | tf_op jit(solution)/shard_map/ppermute | solution.py:351
